TPU v7x, 256 devices: a whole 4x4x8 slice. The times are simulated.
256 devices in a mesh: pb: 16 (over z, core), pa: 16 (over y, x).
Axes of the slice: x: 4, y: 4, z: 8, core: 2. Of those that a mesh axis runs over, the one named last changes fastest.
Arguments:
- query_hidden: bfloat16 [4096, 32, 4096], P(('pb', 'pa')), may hold values from -6 to 6
- passage_hidden: bfloat16 [768, 256, 4096], P(('pb', 'pa')), may hold values from -6 to 6
- projection: bfloat16 [4096, 128], replicated, may hold values from -0.09375 to 0.09375
- candidates: int32 [4096, 9], P(('pb', 'pa')), may hold values from 0 to 47, all different within a row; in each aligned block of 16 rows (0 to 15, 16 to 31, ...) at most 5 rows name the same one
Outputs:
- query_loss: float32 [4096], P(('pb', 'pa'))
- query_grad: float32 [4096, 32, 128], P(('pb', 'pa'))
- passage_grad: float32 [768, 256, 128], P(('pb', 'pa'))
- weight_grad: float32 [4096, 128], replicated
Inputs may be any that keep to these rules, and one draw needn't show every extreme that they name: `candidates`: the 9 numbers of a query are different. Among the 16 queries of one device (aligned blocks of rows) no passage is named more than 5 times, and in every draw some passage is named exactly 5 times by some device's queries.
All inputs are finite; a program needn't handle non-finite values.
Results may differ from a plain program's by a relative error of at most 0.015.
Values may be sent and summed in bfloat16 or wider, within the bound.
A program may use at most 128 MiB of HBM per device.

v0:
```python
import jax
import jax.numpy as jnp
from jax import lax
from jax.sharding import PartitionSpec as P

sharpness_divisor = 0.1
epsilon = 1e-06


def project_rows(hidden, projection):
    flattened = hidden.reshape(-1, hidden.shape[-1])
    embedded = jnp.dot(flattened, projection, preferred_element_type=jnp.float32)
    inv_norm = lax.rsqrt(jnp.mean(embedded * embedded, axis=-1, keepdims=True) + epsilon)
    return (embedded, inv_norm, (embedded * inv_norm).astype(jnp.bfloat16))


def norm_backward(embedded, inv_norm, unit_grad):
    inner_mean = jnp.mean(embedded * unit_grad, axis=-1, keepdims=True)
    return inv_norm * unit_grad - inv_norm * inv_norm * inv_norm * embedded * inner_mean


def contrast_loss(pairwise_similarity, positive):
    exponent = jnp.exp(pairwise_similarity)
    element_total = jnp.sum(exponent, axis=-1, keepdims=True)
    query_loss = jnp.log(element_total[:, 0]) - pairwise_similarity[:, 0]
    return (query_loss, exponent / element_total - positive)


def shards(query_hidden, passage_hidden, projection, candidates):
    query_count, query_len, feature_width = query_hidden.shape
    passage_count, passage_len, _ = passage_hidden.shape
    vector_dimension = projection.shape[1]
    cand_count = candidates.shape[1]
    shard_count = lax.axis_size("pa")
    group_total = passage_count * shard_count
    q_embed, q_norm, q_unit = project_rows(query_hidden, projection)
    p_embed, p_norm, p_unit = project_rows(passage_hidden, projection)
    passage_units = p_unit.reshape(passage_count, passage_len, vector_dimension)
    positive = (jnp.arange(cand_count) == 0).astype(jnp.float32)
    flat_ids = candidates.reshape(-1)
    divisor_total = vector_dimension * sharpness_divisor
    slot_most = max(
        2,
        min(query_count, (3 * query_count * cand_count + 2 * group_total - 1) // (2 * group_total)),
    )
    slot_count = group_total * slot_most
    marks = (flat_ids[:, None] == jnp.arange(group_total, dtype=jnp.int32)[None, :]).astype(
        jnp.int32
    )
    earlier = jnp.sum((jnp.cumsum(marks, axis=0) - marks) * marks, axis=1)
    slot_index = flat_ids * slot_most + earlier
    dispatch = (jnp.arange(slot_count, dtype=jnp.int32)[:, None] == slot_index[None, :]).astype(
        jnp.float32
    )
    by_query = jnp.sum(dispatch.reshape(slot_count, query_count, cand_count), axis=2)
    outgoing = jnp.dot(
        by_query.astype(jnp.bfloat16),
        q_unit.reshape(query_count, query_len * vector_dimension),
        preferred_element_type=jnp.float32,
    ).astype(jnp.bfloat16)
    outgoing = outgoing.reshape(
        shard_count, passage_count * slot_most, query_len * vector_dimension
    )
    arrived = lax.all_to_all(outgoing, "pa", split_axis=0, concat_axis=0, tiled=True)
    arrived = arrived.reshape(shard_count, passage_count, slot_most, query_len, vector_dimension)
    affinity_values = (
        jnp.einsum("spmie,pje->spmij", arrived, passage_units, preferred_element_type=jnp.float32)
        / divisor_total
    )
    exponent = jnp.exp(affinity_values)
    element_total = jnp.sum(exponent, axis=-1, keepdims=True)
    weights = exponent / element_total
    passage_position_affinity = sharpness_divisor * jnp.sum(jnp.log(element_total[..., 0]), axis=-1)
    returned = lax.all_to_all(
        passage_position_affinity.reshape(shard_count, passage_count * slot_most),
        "pa",
        split_axis=0,
        concat_axis=0,
        tiled=True,
    )
    pairwise_similarity = jnp.dot(
        returned.reshape(slot_count), dispatch, precision=lax.Precision.HIGHEST
    ).reshape(query_count, cand_count)
    query_loss, grad_score = contrast_loss(pairwise_similarity, positive)
    slot_grad = jnp.dot(dispatch, grad_score.reshape(-1), precision=lax.Precision.HIGHEST)
    slot_back = lax.all_to_all(
        slot_grad.reshape(shard_count, passage_count * slot_most),
        "pa",
        split_axis=0,
        concat_axis=0,
        tiled=True,
    )
    slot_back = slot_back.reshape(shard_count, passage_count, slot_most)
    weighted = (slot_back[..., None, None] * weights / vector_dimension).astype(jnp.bfloat16)
    slot_query = jnp.einsum(
        "spmij,pje->spmie", weighted, passage_units, preferred_element_type=jnp.float32
    )
    grad_p = jnp.einsum("spmij,spmie->pje", weighted, arrived, preferred_element_type=jnp.float32)
    returned_grads = lax.all_to_all(
        slot_query.reshape(
            shard_count, passage_count * slot_most, query_len * vector_dimension
        ).astype(jnp.bfloat16),
        "pa",
        split_axis=0,
        concat_axis=0,
        tiled=True,
    ).astype(jnp.float32)
    grad_q = lax.dot_general(
        by_query,
        returned_grads.reshape(slot_count, query_len * vector_dimension),
        (((0,), (0,)), ((), ())),
        precision=lax.Precision.HIGHEST,
    )
    query_grad = norm_backward(q_embed, q_norm, grad_q.reshape(-1, vector_dimension))
    passage_grad = norm_backward(p_embed, p_norm, grad_p.reshape(-1, vector_dimension))
    contract = (((0,), (0,)), ((), ()))
    local_sum = lax.dot_general(
        query_hidden.reshape(-1, feature_width),
        query_grad.astype(jnp.bfloat16),
        contract,
        preferred_element_type=jnp.float32,
    )
    local_sum = local_sum + lax.dot_general(
        passage_hidden.reshape(-1, feature_width),
        passage_grad.astype(jnp.bfloat16),
        contract,
        preferred_element_type=jnp.float32,
    )
    weight_grad = lax.psum(local_sum, ("pb", "pa"))
    return (
        query_loss,
        query_grad.reshape(query_count, query_len, vector_dimension),
        passage_grad.reshape(passage_count, passage_len, vector_dimension),
        weight_grad,
    )


def solution(mesh):
    placed = (P(("pb", "pa"), None, None), P(("pb", "pa"), None, None), P(), P(("pb", "pa"), None))
    return jax.shard_map(
        shards,
        mesh=mesh,
        in_specs=placed,
        out_specs=(P(("pb", "pa")), P(("pb", "pa"), None, None), P(("pb", "pa"), None, None), P()),
        check_vma=False,
    )
```

profile of v0, /device:TPU:1, one launch (start us, length us, event | category | flops | bytes accessed | tf_op | source)
XLA Modules:
  0.0 419.1 jit_solution(5674458891738921514)
XLA Ops:
  7.2 0.9 eq.76
  8.1 0.6 reduce-window.6
  8.7 0.2 slice_reduce_fusion
  8.9 0.1 bitcast_bitcast_fusion
  9.0 0.1 reduce_sum.85
  9.1 0.7 multiply_add_fusion.1
  9.8 0.1 copy.61
  9.9 0.1 convert_reduce_fusion
  10.0 3.5 multiply_reduce_fusion.2
  13.6 0.6 multiply_multiply_fusion.1
  14.3 0.1 multiply_convert_fusion.1
  14.4 0.4 copy-done.12
  14.8 0.1 reshape.196
  14.9 0.7 convolution_convert_fusion
  15.6 1.6 reshape.197
  17.2 7.6 %all-to-all-start = ((bf16[16,15,4096]{2,1,0:T(8,128)(2,1)}), bf16[16,15,4096]{2,1,0:T(8,128)(2,1)S(1)}, u32[]{:S(2)}, u32[]{:S(2)}) async-start(bf16[16,15,4096]{2,1,0:T(8,128)(2,1)} %reshape.197), calls=%async_computation | async-start | bytes 4194304 | tf_op jit(solution)/shard_map/all_to_all | solution.py:64
  24.8 0.6 multiply_add_fusion
  25.4 4.7 %multiply_reduce_fusion = (f32[768]{0:T(1024)S(1)}, f32[768,128]{1,0:T(8,128)S(1)}) fusion(bf16[768,4096]{1,0:T(8,128)(2,1)} %bitcast.73, bf16[4096,128]{1,0:T(8,128)(2,1)S(1)} %copy-done), kind=kOutput, calls=%fused_computation.20 | convolution fusion | flops 805502208 | bytes 7736320 | tf_op jit(solution)/shard_map/dot_general | solution.py:12
  30.1 0.6 multiply_multiply_fusion
  30.7 0.7 iota_compare_fusion
  31.4 0.8 multiply_convert_fusion
  32.2 23.1 %all-to-all-done = bf16[16,15,4096]{2,1,0:T(8,128)(2,1)S(1)} async-done(((bf16[16,15,4096]{2,1,0:T(8,128)(2,1)}), bf16[16,15,4096]{2,1,0:T(8,128)(2,1)S(1)}, u32[]{:S(2)}, u32[]{:S(2)}) %all-to-all-start) | async-done | bytes 1966112 | tf_op jit(solution)/shard_map/all_to_all | solution.py:64
  55.3 2.7 reshape.213
  58.0 6.2 %bitcast_reduce_fusion = (f32[16,3,5,32]{3,2,0,1:T(8,128)S(1)}, f32[3,256,16,5,32]{1,4,3,2,0:T(8,128)}) fusion(bf16[3,256,128,1,1]{2,1,4,3,0:T(8,128)(2,1)} %bitcast.81, bf16[16,3,5,32,128]{4,3,2,1,0:T(8,128)(2,1)} %reshape.213), kind=kOutput, calls=%fused_computation.1 | convolution fusion | flops 507240960 | bytes 10057728 | tf_op jit(solution)/shard_map/spmie,pje->spmij/dot_general | solution.py:67
  64.2 0.1 log_reduce_fusion
  64.3 0.1 copy.65
  64.4 0.7 copy.66
  65.1 4.3 %all-to-all-start.1 = ((f32[16,1,15]{2,1,0:T(1,128)}), f32[16,1,15]{2,1,0:T(1,128)S(1)}, u32[]{:S(2)}, u32[]{:S(2)}) async-start(f32[16,1,15]{2,1,0:T(1,128)} %copy.66), calls=%async_computation.1 | async-start | bytes 16384 | tf_op jit(solution)/shard_map/all_to_all | solution.py:74
  69.4 6.3 %all-to-all-done.1 = f32[16,1,15]{2,1,0:T(1,128)S(1)} async-done(((f32[16,1,15]{2,1,0:T(1,128)}), f32[16,1,15]{2,1,0:T(1,128)S(1)}, u32[]{:S(2)}, u32[]{:S(2)}) %all-to-all-start.1) | async-done | bytes 992 | tf_op jit(solution)/shard_map/all_to_all | solution.py:74
  75.7 0.5 broadcast.150
  76.2 0.7 reduce.7
  76.9 0.1 reshape.208
  77.0 0.6 fusion.19
  77.5 0.1 exponential_reduce_fusion
  77.7 0.1 divide_subtract_fusion
  77.8 0.4 copy-done.17
  78.2 0.1 reshape.210
  78.3 0.6 convolution_bitcast_fusion
  78.9 9.1 %all_to_all.25 = f32[16,1,15]{2,1,0:T(1,128)S(1)} all-to-all(f32[16,1,15]{2,1,0:T(1,128)S(1)} %convolution_bitcast_fusion), channel_id=1, replica_groups=mesh['pb'=16,'pa'=16] {'pa'}, dimensions={0} | all-to-all | bytes 1920 | tf_op jit(solution)/shard_map/all_to_all | solution.py:86
  88.1 0.1 copy.67
  88.1 0.1 copy.68
  88.2 5.0 %fusion.2 = bf16[16,3,5,32,256]{4,3,2,0,1:T(8,128)(2,1)S(1)} fusion(f32[3,256,16,5,32]{1,4,3,2,0:T(8,128)} %get-tuple-element.37, f32[16,3,5,32]{3,2,0,1:T(8,128)S(1)} %get-tuple-element.36, f32[16,3,5]{2,0,1:T(8,128)S(1)} %copy.68), kind=kLoop, calls=%fused_computation.4 | loop fusion | flops 9830400 | bytes 11828160 | tf_op jit(solution)/shard_map/convert_element_type | solution.py:94
  93.2 1.2 convert_bitcast_fusion
  94.4 0.7 copy-done.2
  95.1 1.6 copy.80
  96.7 4.3 %reshape.216 = bf16[16,15,4096]{2,1,0:T(8,128)(2,1)} reshape(bf16[16,3,5,32,128]{4,3,2,1,0:T(8,128)(2,1)} %copy.80) | data formatting | bytes 3932160 | tf_op jit(solution)/shard_map/convert_element_type | solution.py:102
  101.1 4.4 %all-to-all-start.3 = ((bf16[16,15,4096]{2,1,0:T(8,128)(2,1)}), bf16[16,15,4096]{2,1,0:T(8,128)(2,1)}, u32[]{:S(2)}, u32[]{:S(2)}) async-start(bf16[16,15,4096]{2,1,0:T(8,128)(2,1)} %reshape.216), calls=%async_computation.3 | async-start | bytes 4194304 | tf_op jit(solution)/shard_map/all_to_all | solution.py:99
  105.5 0.2 all-reduce.3.cloned.1.call-start
  105.8 3.6 fusion.4
  109.4 0.2 fusion.9
  109.6 1.1 fusion.8
  110.7 19.6 %all-to-all-done.3 = bf16[16,15,4096]{2,1,0:T(8,128)(2,1)} async-done(((bf16[16,15,4096]{2,1,0:T(8,128)(2,1)}), bf16[16,15,4096]{2,1,0:T(8,128)(2,1)}, u32[]{:S(2)}, u32[]{:S(2)}) %all-to-all-start.3) | async-done | bytes 1966112 | tf_op jit(solution)/shard_map/all_to_all | solution.py:99
  130.3 3.0 reshape.201
  133.3 2.4 fusion.20
  135.7 0.8 reshape.202
  136.5 1.3 multiply_reduce_fusion.1
  137.8 1.5 multiply_subtract_fusion
  139.3 0.7 copy-done.5
  140.0 2.9 fusion.12
  143.0 2.4 fusion.3
  145.4 0.1 slice_reduce_fusion.1
  145.6 0.5 log_subtract_fusion
  146.1 263.3 %all-reduce.3.cloned.1.call-done = f32[4096,128]{0,1:T(8,128)} async-done(((f32[4096,128]{0,1:T(8,128)}), f32[4096,128]{0,1:T(8,128)}) %all-reduce.3.cloned.1.call-update) | async-done | bytes 2097168 | tf_op jit(solution)/shard_map/psum | solution.py:129
  409.4 2.9 copy.73
  (53 shorter events, 0.3 us)
Async XLA Ops:
  7.2 2.9 copy-start
  13.5 0.7 copy-start.4
  14.2 0.6 copy-start.12
  17.2 38.1 %all-to-all-start = ((bf16[16,15,4096]{2,1,0:T(8,128)(2,1)}), bf16[16,15,4096]{2,1,0:T(8,128)(2,1)S(1)}, u32[]{:S(2)}, u32[]{:S(2)}) async-start(bf16[16,15,4096]{2,1,0:T(8,128)(2,1)} %reshape.197), calls=%async_computation | async-start | bytes 4194304 | tf_op jit(solution)/shard_map/all_to_all | solution.py:64
  25.4 5.3 %copy-start.15 = (s32[144]{0:T(256)}, s32[144]{0:T(256)S(1)}, u32[]{:S(2)}) copy-start(s32[144]{0:T(256)S(1)} %multiply_add_fusion.2) | copy-start | bytes 1732
  30.7 0.7 copy-start.10
  58.0 11.4 %copy-start.7 = (pred[144,240]{1,0:T(8,128)(4,1)S(1)}, pred[144,240]{1,0:T(8,128)(4,1)}, u32[]{:S(2)}) copy-start(pred[144,240]{1,0:T(8,128)(4,1)} %iota_compare_fusion) | copy-start | bytes 103684
  58.0 20.3 %copy-start.14 = (s32[16,15]{1,0:T(8,128)S(1)}, s32[16,15]{1,0:T(8,128)}, u32[]{:S(2)}) copy-start(s32[16,15]{1,0:T(8,128)} %multiply_add_fusion) | copy-start | bytes 2884
  58.0 20.3 %copy-start.16 = (s32[144]{0:T(256)S(1)}, s32[144]{0:T(256)}, u32[]{:S(2)}) copy-start(s32[144]{0:T(256)} %copy-done.15) | copy-start | bytes 1732
  65.1 10.6 %all-to-all-start.1 = ((f32[16,1,15]{2,1,0:T(1,128)}), f32[16,1,15]{2,1,0:T(1,128)S(1)}, u32[]{:S(2)}, u32[]{:S(2)}) async-start(f32[16,1,15]{2,1,0:T(1,128)} %copy.66), calls=%async_computation.1 | async-start | bytes 16384 | tf_op jit(solution)/shard_map/all_to_all | solution.py:74
  77.5 10.7 %copy-start.8 = (f32[1,16,9]{2,0,1:T(1,128)}, f32[1,16,9]{2,0,1:T(1,128)S(1)}, u32[]{:S(2)}) copy-start(f32[1,16,9]{2,0,1:T(1,128)S(1)} %fusion.19) | copy-start | bytes 1732
  77.7 0.5 copy-start.17
  88.2 5.0 %copy-start.6 = (bf16[768,128]{1,0:T(8,128)(2,1)S(1)}, bf16[768,128]{1,0:T(8,128)(2,1)}, u32[]{:S(2)}) copy-start(bf16[768,128]{1,0:T(8,128)(2,1)} %multiply_convert_fusion) | copy-start | bytes 589828
  93.2 1.9 copy-start.2
  96.7 9.0 %copy-start.1 = (bf16[16,3,5,32,128]{4,3,2,1,0:T(8,128)(2,1)S(1)}, bf16[16,3,5,32,128]{4,3,2,1,0:T(8,128)(2,1)}, u32[]{:S(2)}) copy-start(bf16[16,3,5,32,128]{4,3,2,1,0:T(8,128)(2,1)} %reshape.213) | copy-start | bytes 5898244
  101.1 29.3 %all-to-all-start.3 = ((bf16[16,15,4096]{2,1,0:T(8,128)(2,1)}), bf16[16,15,4096]{2,1,0:T(8,128)(2,1)}, u32[]{:S(2)}, u32[]{:S(2)}) async-start(bf16[16,15,4096]{2,1,0:T(8,128)(2,1)} %reshape.216), calls=%async_computation.3 | async-start | bytes 4194304 | tf_op jit(solution)/shard_map/all_to_all | solution.py:99
  105.5 4.0 copy-start.11
  105.5 4.0 copy-start.13
  105.5 303.9 %all-reduce.3.cloned.1.call-start = ((), (), s32[]{:S(2)}) async-start(), calls=%async_computation.4 | async-start | bytes 4194304 | tf_op jit(solution)/shard_map/psum | solution.py:129
  130.3 12.6 %slice-start = ((s8[6291456]{0:T(1024)(128)(4,1)}), s8[2097152]{0:T(1024)(128)(4,1)S(1)}, s32[]{:S(2)}) async-start(s8[6291456]{0:T(1024)(128)(4,1)} %bitcast.74), calls=%async_computation.5 | async-start | bytes 4194304
  136.5 6.5 %slice-start.1 = ((s8[6291456]{0:T(1024)(128)(4,1)}), s8[4194304]{0:T(1024)(128)(4,1)S(1)}, s32[]{:S(2)}) async-start(s8[6291456]{0:T(1024)(128)(4,1)} %bitcast.74), calls=%async_computation.6 | async-start | bytes 8388608
  136.5 6.5 %copy-start.3 = (f32[768,128]{1,0:T(8,128)S(1)}, f32[768,128]{1,0:T(8,128)}, u32[]{:S(2)}) copy-start(f32[768,128]{1,0:T(8,128)} %fusion.8) | copy-start | bytes 1179652
  139.3 0.7 copy-start.5
  143.0 2.4 copy-start.9
  143.0 2.5 copy-start.18
Sparse Core Ops, SparseCore 0:
  145.6 263.8 all-reduce.2
where the time goes:
time: 420 us; the launch traced here: 419 us
  waiting for transfers between devices  312 us (74%)
  matrix products  28.7 us (7%)
  local copies, waits for them, and re-layouts  22.3 us (5%)
  starting transfers between devices  16.5 us (4%)
  other arithmetic  15.7 us (4%)
  between operations  14.4 us (3%)
  blocking collectives  9.11 us (2%)
    psum x1, waiting for transfers between devices, shards(): weight_grad = lax.psum(local_sum, ('pb', 'pa'))  263 us
    all_to_all x1, waiting for transfers between devices, shards(): lax.all_to_all(outgoing, 'pa', split_axis=0, concat_axis=0, tiled=True)  23.1 us
    all_to_all x1, waiting for transfers between devices, shards(): lax.all_to_all(slot_query.reshape(shard_count, passage_count * slot_most,...  19.6 us
    all_to_all x1, blocking collectives, shards(): lax.all_to_all(slot_grad.reshape(shard_count, passage_count * slot_most),...  9.11 us
  transfers between devices with their start and end apart: 4, of which 4 were waited for; matrix products, arithmetic and copies ran while one was open for 3% of the time, Pallas kernels for 0%

commit v1 on v0

--- a/solution.py
+++ b/solution.py
@@ -1,7 +1,174 @@
+import functools
 import jax
 import jax.numpy as jnp
 from jax import lax
+from jax.experimental import pallas as pl
+from jax.experimental.pallas import tpu as pltpu
+
 from jax.sharding import PartitionSpec as P
+
+MESH = pl.DeviceIdType.MESH
+F32, BF16 = jnp.float32, jnp.bfloat16
+
+
+def remote(src, dst, send, recv, device):
+    return pltpu.make_async_remote_copy(
+        src_ref=src, dst_ref=dst, send_sem=send, recv_sem=recv, device_id=device, device_id_type=MESH
+    )
+
+
+def sum_kernel(n_pa, n_z, g_ref, o_ref, out, half, got0, part, got1, mine, got2,
+               s0, r0, s1, r1, s2, r2, s3, r3, s4, r4, s5, r5):
+    rows = g_ref.shape[0]
+    half_rows = rows // 2
+    chunk = half_rows // n_pa
+    piece = chunk // n_z
+    pa, pb = lax.axis_index("pa"), lax.axis_index("pb")
+    z, core = pb // 2, pb % 2
+    partner = {"pb": z * 2 + (1 - core)}
+    base = core * half_rows
+
+    def xy(k):
+        return lax.rem(pa + k, n_pa)
+
+    def zz(k):
+        return lax.rem(z + k, n_z)
+
+    barrier = pltpu.get_barrier_semaphore()
+    pl.semaphore_signal(barrier, inc=1, device_id=partner, device_id_type=MESH)
+
+    @pl.loop(1, n_pa)
+    def _(k):
+        pl.semaphore_signal(barrier, inc=1, device_id={"pa": xy(k)}, device_id_type=MESH)
+
+    @pl.loop(1, n_z)
+    def _(k):
+        pl.semaphore_signal(barrier, inc=1, device_id={"pb": zz(k) * 2 + core}, device_id_type=MESH)
+
+    half[...] = g_ref[pl.ds((1 - core) * half_rows, half_rows), :].astype(BF16)
+    pl.semaphore_wait(barrier, n_pa + n_z - 1)
+
+    def swap(k):
+        at = pl.ds(xy(k) * chunk, chunk)
+        return remote(half.at[at], got0.at[at], s0.at[k], r0.at[k], partner)
+
+    def to_xy(k):
+        return remote(part.at[xy(k)], got1.at[pa], s1.at[k], r1.at[n_pa - k], {"pa": xy(k)})
+
+    @pl.loop(0, n_pa)
+    def _(k):
+        swap(lax.rem(k + 1, n_pa)).start()
+
+    @pl.loop(1, n_pa)
+    def _(k):
+        peer = xy(k)
+        swap(k).wait_recv()
+        mix = g_ref[pl.ds(base + peer * chunk, chunk), :] + got0[pl.ds(peer * chunk, chunk), :].astype(F32)
+        part[peer] = mix.astype(BF16)
+        to_xy(k).start()
+
+    swap(0).wait_recv()
+    mine[...] = g_ref[pl.ds(base + pa * chunk, chunk), :] + got0[pl.ds(pa * chunk, chunk), :].astype(F32)
+
+    @pl.loop(1, n_pa)
+    def _(k):
+        remote(part.at[xy(k)], got1.at[xy(k)], s1.at[k], r1.at[k], {"pa": xy(k)}).wait_recv()
+        mine[...] += got1[xy(k)].astype(F32)
+
+    part[pa] = mine[...].astype(BF16)
+
+    def to_z(k):
+        return remote(part.at[pa, pl.ds(zz(k) * piece, piece)], got2.at[z], s2.at[k], r2.at[n_z - k],
+                      {"pb": zz(k) * 2 + core})
+
+    @pl.loop(1, n_z)
+    def _(k):
+        to_z(k).start()
+
+    total = mine[pl.ds(z * piece, piece), :]
+    for k in range(1, n_z):
+        remote(part.at[pa, pl.ds(0, piece)], got2.at[zz(k)], s2.at[k], r2.at[k], {"pb": zz(k) * 2 + core}).wait_recv()
+        total = total + got2[zz(k)].astype(F32)
+    at_z = pl.ds(base + pa * chunk + z * piece, piece)
+    out[at_z, :] = total.astype(BF16)
+
+    def back_z(k, who):
+        at = pl.ds(base + pa * chunk + who * piece, piece)
+        return remote(out.at[at], out.at[at], s3.at[k], r3.at[n_z - k], {"pb": zz(k) * 2 + core})
+
+    @pl.loop(1, n_z)
+    def _(k):
+        back_z(k, z).start()
+
+    @pl.loop(1, n_z)
+    def _(k):
+        at = pl.ds(base + pa * chunk + zz(k) * piece, piece)
+        remote(out.at[at], out.at[at], s3.at[k], r3.at[k], {"pb": zz(k) * 2 + core}).wait_recv()
+
+    at_pa = pl.ds(base + pa * chunk, chunk)
+
+    @pl.loop(1, n_pa)
+    def _(k):
+        remote(out.at[at_pa], out.at[at_pa], s4.at[k], r4.at[n_pa - k], {"pa": xy(k)}).start()
+
+    def across(k, first):
+        at = pl.ds(first + xy(k) * chunk, chunk)
+        return remote(out.at[at], out.at[at], s5.at[k], r5.at[k], partner)
+
+    across(0, base).start()
+
+    @pl.loop(1, n_pa)
+    def _(k):
+        at = pl.ds(base + xy(k) * chunk, chunk)
+        remote(out.at[at], out.at[at], s4.at[k], r4.at[k], {"pa": xy(k)}).wait_recv()
+        across(k, base).start()
+
+    @pl.loop(0, n_pa)
+    def _(k):
+        across(k, half_rows - base).wait_recv()
+
+    @pl.loop(0, n_pa)
+    def _(k):
+        swap(k).wait_send()
+        across(k, base).wait_send()
+
+    @pl.loop(1, n_pa)
+    def _(k):
+        to_xy(k).wait_send()
+        remote(out.at[at_pa], out.at[at_pa], s4.at[k], r4.at[k], {"pa": xy(k)}).wait_send()
+
+    @pl.loop(1, n_z)
+    def _(k):
+        to_z(k).wait_send()
+        back_z(k, z).wait_send()
+
+    o_ref[...] = out[...]
+
+
+def sum_all(g, n_pa, n_z):
+    rows, width = g.shape
+    chunk = rows // 2 // n_pa
+    piece = chunk // n_z
+    dma = pltpu.SemaphoreType.DMA
+    return pl.pallas_call(
+        functools.partial(sum_kernel, n_pa, n_z),
+        out_shape=jax.ShapeDtypeStruct((rows, width), BF16),
+        in_specs=[pl.BlockSpec(memory_space=pltpu.VMEM)],
+        out_specs=pl.BlockSpec(memory_space=pltpu.VMEM),
+        scratch_shapes=[
+            pltpu.VMEM((rows, width), BF16),
+            pltpu.VMEM((rows // 2, width), BF16),
+            pltpu.VMEM((rows // 2, width), BF16),
+            pltpu.VMEM((n_pa, chunk, width), BF16),
+            pltpu.VMEM((n_pa, chunk, width), BF16),
+            pltpu.VMEM((chunk, width), F32),
+            pltpu.VMEM((n_z, piece, width), BF16),
+            dma((n_pa,)), dma((n_pa,)), dma((n_pa,)), dma((n_pa,)), dma((n_z,)), dma((n_z,)),
+            dma((n_z,)), dma((n_z,)), dma((n_pa,)), dma((n_pa,)), dma((n_pa,)), dma((n_pa,)),
+        ],
+        compiler_params=pltpu.CompilerParams(collective_id=0, has_side_effects=True, vmem_limit_bytes=32 * 2**20),
+        name="sum_devices",
+    )(g)
 
 sharpness_divisor = 0.1
 epsilon = 1e-06
@@ -126,7 +293,7 @@
         contract,
         preferred_element_type=jnp.float32,
     )
-    weight_grad = lax.psum(local_sum, ("pb", "pa"))
+    weight_grad = sum_all(local_sum, lax.axis_size("pa"), lax.axis_size("pb") // 2).astype(F32)
     return (
         query_loss,
         query_grad.reshape(query_count, query_len, vector_dimension),

time: 420 us -> 179 us (0.43)
  waiting for transfers between devices: 312 us -> 46.4 us
  Pallas kernels: 0 us -> 42.4 us
  between operations: 14.4 us -> 1 us
  local copies, waits for them, and re-layouts: 22.3 us -> 15.4 us
  matrix products: 28.7 us -> 33.1 us
    psum x1 -> x0, waiting for transfers between devices: 263 us -> none  [shards(): weight_grad = lax.psum(local_sum, ('pb', 'pa'))]
    pallas_call x0 -> x1, Pallas kernels: none -> 42.4 us  [sum_all(): pl.pallas_call(functools.partial(sum_kernel, n_pa, n_z), out_shape=jax.Sh...]
  transfers between devices with their start and end apart: 4 -> 3, of which waited for: 4 -> 3; matrix products, arithmetic and copies ran while one was open for 3% -> 8% of each run, Pallas kernels for 0% -> 0%
where the time goes in v1:
time: 179 us
  waiting for transfers between devices  46.4 us (26%)
  Pallas kernels  42.4 us (24%)
  matrix products  33.1 us (18%)
  starting transfers between devices  15.8 us (9%)
  local copies, waits for them, and re-layouts  15.4 us (9%)
  other arithmetic  15.4 us (9%)
  blocking collectives  9.11 us (5%)
    pallas_call x1, Pallas kernels, sum_all(): pl.pallas_call(functools.partial(sum_kernel, n_pa, n_z), out_shape=jax.Sh...  42.4 us
    all_to_all x1, waiting for transfers between devices, shards(): lax.all_to_all(outgoing, 'pa', split_axis=0, concat_axis=0, tiled=True)  23.1 us
    all_to_all x1, waiting for transfers between devices, shards(): lax.all_to_all(slot_query.reshape(shard_count, passage_count * slot_most,...  17.1 us
    all_to_all x1, blocking collectives, shards(): lax.all_to_all(slot_grad.reshape(shard_count, passage_count * slot_most),...  9.11 us
    dot_general x2, matrix products, project_rows(): jnp.dot(flattened, projection, preferred_element_type=jnp.float32)  8.17 us
    all_to_all x1, starting transfers between devices, shards(): lax.all_to_all(outgoing, 'pa', split_axis=0, concat_axis=0, tiled=True)  7.58 us
    all_to_all x1, waiting for transfers between devices, shards(): lax.all_to_all(passage_position_affinity.reshape(shard_count, passage_cou...  6.26 us
    dot_general x1, matrix products, shards(): jnp.einsum('spmie,pje->spmij', arrived, passage_units, preferred_element_...  6.17 us
  transfers between devices with their start and end apart: 3, of which 3 were waited for; matrix products, arithmetic and copies ran while one was open for 8% of the time, Pallas kernels for 0%

profile of v1, /device:TPU:1, one launch (start us, length us, event | category | flops | bytes accessed | tf_op | source)
XLA Modules:
  0.0 178.6 jit_solution(12879070280973943545)
XLA Ops:
  0.6 0.0 copy-start
  0.6 0.9 eq.76
  1.6 0.6 reduce-window.6
  2.2 0.2 slice_reduce_fusion
  2.4 0.1 bitcast_bitcast_fusion
  2.5 0.1 reduce_sum.85
  2.6 0.7 multiply_add_fusion.1
  3.3 0.1 copy.66
  3.4 0.1 convert_reduce_fusion
  3.5 3.5 %multiply_reduce_fusion.2 = (f32[512]{0:T(512)S(1)}, f32[512,128]{1,0:T(8,128)S(1)}) fusion(bf16[512,4096]{1,0:T(8,128)(2,1)} %bitcast.75, bf16[4096,128]{1,0:T(8,128)(2,1)S(1)} %copy-done), kind=kOutput, calls=%fused_computation.24 | convolution fusion | flops 537001472 | bytes 5507072 | tf_op jit(solution)/shard_map/dot_general | solution.py:179
  7.0 0.6 multiply_multiply_fusion.1
  7.7 0.1 copy-done.2
  7.7 0.1 multiply_convert_fusion.1
  7.9 0.4 copy-done.11
  8.3 0.1 reshape.196
  8.3 0.7 convolution_convert_fusion
  9.0 1.6 reshape.197
  10.7 7.6 %all-to-all-start = ((bf16[16,15,4096]{2,1,0:T(8,128)(2,1)}), bf16[16,15,4096]{2,1,0:T(8,128)(2,1)S(1)}, u32[]{:S(2)}, u32[]{:S(2)}) async-start(bf16[16,15,4096]{2,1,0:T(8,128)(2,1)} %reshape.197), calls=%async_computation | async-start | bytes 4194304 | tf_op jit(solution)/shard_map/all_to_all | solution.py:231
  18.3 0.6 multiply_add_fusion
  18.9 4.7 %multiply_reduce_fusion = (f32[768]{0:T(1024)S(1)}, f32[768,128]{1,0:T(8,128)S(1)}) fusion(bf16[768,4096]{1,0:T(8,128)(2,1)} %bitcast.73, bf16[4096,128]{1,0:T(8,128)(2,1)S(1)} %copy-done), kind=kOutput, calls=%fused_computation.20 | convolution fusion | flops 805502208 | bytes 7736320 | tf_op jit(solution)/shard_map/dot_general | solution.py:179
  23.5 0.6 multiply_multiply_fusion
  24.1 0.7 iota_compare_fusion
  24.8 0.8 multiply_convert_fusion
  25.7 23.1 %all-to-all-done = bf16[16,15,4096]{2,1,0:T(8,128)(2,1)S(1)} async-done(((bf16[16,15,4096]{2,1,0:T(8,128)(2,1)}), bf16[16,15,4096]{2,1,0:T(8,128)(2,1)S(1)}, u32[]{:S(2)}, u32[]{:S(2)}) %all-to-all-start) | async-done | bytes 1966112 | tf_op jit(solution)/shard_map/all_to_all | solution.py:231
  48.7 2.7 %reshape.213 = bf16[16,3,5,32,128]{4,3,2,1,0:T(8,128)(2,1)} reshape(bf16[16,15,4096]{2,1,0:T(8,128)(2,1)S(1)} %all-to-all-done) | data formatting | bytes 3932160 | tf_op jit(solution)/shard_map/reshape | solution.py:232
  51.4 6.2 %bitcast_reduce_fusion = (f32[16,3,5,32]{3,2,0,1:T(8,128)S(1)}, f32[3,256,16,5,32]{1,4,3,2,0:T(8,128)}) fusion(bf16[3,256,128,1,1]{2,1,4,3,0:T(8,128)(2,1)} %bitcast.79, bf16[16,3,5,32,128]{4,3,2,1,0:T(8,128)(2,1)} %reshape.213), kind=kOutput, calls=%fused_computation.1 | convolution fusion | flops 507240960 | bytes 10057728 | tf_op jit(solution)/shard_map/spmie,pje->spmij/dot_general | solution.py:234
  57.6 0.1 log_reduce_fusion
  57.8 0.1 copy.70
  57.9 0.7 copy.71
  58.5 4.3 %all-to-all-start.1 = ((f32[16,1,15]{2,1,0:T(1,128)}), f32[16,1,15]{2,1,0:T(1,128)S(1)}, u32[]{:S(2)}, u32[]{:S(2)}) async-start(f32[16,1,15]{2,1,0:T(1,128)} %copy.71), calls=%async_computation.1 | async-start | bytes 16384 | tf_op jit(solution)/shard_map/all_to_all | solution.py:241
  62.9 6.3 %all-to-all-done.1 = f32[16,1,15]{2,1,0:T(1,128)S(1)} async-done(((f32[16,1,15]{2,1,0:T(1,128)}), f32[16,1,15]{2,1,0:T(1,128)S(1)}, u32[]{:S(2)}, u32[]{:S(2)}) %all-to-all-start.1) | async-done | bytes 992 | tf_op jit(solution)/shard_map/all_to_all | solution.py:241
  69.2 0.5 broadcast.150
  69.7 0.7 reduce.7
  70.3 0.1 reshape.208
  70.4 0.6 fusion.19
  71.0 0.1 exponential_reduce_fusion
  71.1 0.0 copy-start.18
  71.1 0.1 divide_subtract_fusion
  71.2 0.4 copy-done.18
  71.7 0.1 reshape.210
  71.8 0.6 convolution_bitcast_fusion
  72.4 9.1 %all_to_all.25 = f32[16,1,15]{2,1,0:T(1,128)S(1)} all-to-all(f32[16,1,15]{2,1,0:T(1,128)S(1)} %convolution_bitcast_fusion), channel_id=1, replica_groups=mesh['pb'=16,'pa'=16] {'pa'}, dimensions={0} | all-to-all | bytes 1920 | tf_op jit(solution)/shard_map/all_to_all | solution.py:253
  81.5 0.1 copy.72
  81.6 0.1 copy.73
  81.7 5.0 %fusion.2 = bf16[16,3,5,32,256]{4,3,2,0,1:T(8,128)(2,1)S(1)} fusion(f32[3,256,16,5,32]{1,4,3,2,0:T(8,128)} %get-tuple-element.13, f32[16,3,5,32]{3,2,0,1:T(8,128)S(1)} %get-tuple-element.12, f32[16,3,5]{2,0,1:T(8,128)S(1)} %copy.73), kind=kLoop, calls=%fused_computation.4 | loop fusion | flops 9830400 | bytes 11828160 | tf_op jit(solution)/shard_map/convert_element_type | solution.py:261
  86.7 1.9 %copy-done.1 = bf16[16,3,5,32,256]{4,3,2,0,1:T(8,128)(2,1)} copy-done((bf16[16,3,5,32,256]{4,3,2,0,1:T(8,128)(2,1)}, bf16[16,3,5,32,256]{4,3,2,0,1:T(8,128)(2,1)S(1)}, u32[]{:S(2)}) %copy-start.1) | copy-done | bytes 3932184
  88.6 1.2 convert_bitcast_fusion
  89.7 0.3 copy.88
  90.1 2.4 %reshape.216 = bf16[16,15,4096]{2,1,0:T(8,128)(2,1)} reshape(bf16[16,3,5,32,128]{4,3,2,1,0:T(8,128)(2,1)S(1)} %copy.88) | data formatting | bytes 3932160 | tf_op jit(solution)/shard_map/convert_element_type | solution.py:269
  92.5 3.9 %all-to-all-start.3 = ((bf16[16,15,4096]{2,1,0:T(8,128)(2,1)}), bf16[16,15,4096]{2,1,0:T(8,128)(2,1)S(1)}, u32[]{:S(2)}, u32[]{:S(2)}) async-start(bf16[16,15,4096]{2,1,0:T(8,128)(2,1)} %reshape.216), calls=%async_computation.3 | async-start | bytes 4194304 | tf_op jit(solution)/shard_map/all_to_all | solution.py:266
  96.4 0.8 slice_reduce_fusion.1
  97.3 1.2 log_subtract_fusion
  98.4 4.2 %fusion.4 = f32[3,256,128,1,1]{2,1,3,0,4:T(8,128)S(1)} fusion(bf16[16,3,5,32,128]{4,3,2,1,0:T(8,128)(2,1)} %reshape.213, bf16[16,3,5,32,256]{4,3,2,0,1:T(8,128)(2,1)} %copy-done.1), kind=kOutput, calls=%fused_computation.9 | convolution fusion | flops 503316480 | bytes 6291456 | tf_op jit(solution)/shard_map/spmij,spmie->pje/dot_general | solution.py:265
  102.6 0.2 fusion.9
  102.9 1.1 fusion.8
  104.0 17.1 %all-to-all-done.3 = bf16[16,15,4096]{2,1,0:T(8,128)(2,1)S(1)} async-done(((bf16[16,15,4096]{2,1,0:T(8,128)(2,1)}), bf16[16,15,4096]{2,1,0:T(8,128)(2,1)S(1)}, u32[]{:S(2)}, u32[]{:S(2)}) %all-to-all-start.3) | async-done | bytes 1966112 | tf_op jit(solution)/shard_map/all_to_all | solution.py:266
  121.0 1.6 reshape.201
  122.6 2.4 %fusion.20 = f32[16,4096]{1,0:T(8,128)S(1)} fusion(f32[240,16]{0,1:T(8,128)S(1)} %convert_reduce_fusion, bf16[240,4096]{1,0:T(8,128)(2,1)} %reshape.201), kind=kOutput, calls=%fused_computation.62 | convolution fusion | flops 188743680 | bytes 2243584 | tf_op jit(solution)/shard_map/dot_general | solution.py:275
  125.1 0.1 multiply_reduce_fusion.1
  125.3 0.3 multiply_subtract_fusion
  125.6 4.0 %fusion.12 = f32[128,4096]{0,1:T(8,128)S(1)} fusion(bf16[512,4096]{1,0:T(8,128)(2,1)} %bitcast.76, f32[512,128]{1,0:T(8,128)S(1)} %multiply_subtract_fusion), kind=kOutput, calls=%fused_computation.31 | convolution fusion | flops 536936448 | bytes 6553600 | tf_op jit(solution)/shard_map/dot_general | solution.py:284
  129.6 5.1 %fusion.3.g_ref = f32[4096,128]{1,0:T(8,128)S(1)} fusion(f32[128,4096]{0,1:T(8,128)S(1)} %fusion.12, bf16[768,4096]{1,0:T(8,128)(2,1)} %bitcast.74, f32[768,128]{1,0:T(8,128)S(1)} %copy-done.4), kind=kOutput, calls=%fused_computation.8 | convolution fusion | flops 805928960 | bytes 10878976 | tf_op jit(solution)/shard_map/dot_general | solution.py:290
  134.7 42.4 %sum_devices.1 = bf16[4096,128]{1,0:T(8,128)(2,1)S(1)} custom-call(f32[4096,128]{1,0:T(8,128)S(1)} %fusion.3.g_ref), custom_call_target="tpu_custom_call" | custom-call | tf_op jit(solution)/shard_map/sum_devices/pallas_call | solution.py:153
  177.1 1.5 convert_element_type.62
  (46 shorter events, 0.3 us)
Async XLA Ops:
  0.6 2.9 %copy-start = (bf16[4096,128]{1,0:T(8,128)(2,1)S(1)}, bf16[4096,128]{1,0:T(8,128)(2,1)}, u32[]{:S(2)}) copy-start(bf16[4096,128]{1,0:T(8,128)(2,1)} %param.6) | copy-start | bytes 3145732
  7.0 0.7 copy-start.2
  7.7 0.6 copy-start.11
  10.7 38.1 %all-to-all-start = ((bf16[16,15,4096]{2,1,0:T(8,128)(2,1)}), bf16[16,15,4096]{2,1,0:T(8,128)(2,1)S(1)}, u32[]{:S(2)}, u32[]{:S(2)}) async-start(bf16[16,15,4096]{2,1,0:T(8,128)(2,1)} %reshape.197), calls=%async_computation | async-start | bytes 4194304 | tf_op jit(solution)/shard_map/all_to_all | solution.py:231
  18.9 5.3 %copy-start.16 = (s32[144]{0:T(256)}, s32[144]{0:T(256)S(1)}, u32[]{:S(2)}) copy-start(s32[144]{0:T(256)S(1)} %multiply_add_fusion.2) | copy-start | bytes 1732
  24.1 0.7 copy-start.9
  51.4 11.4 %copy-start.7 = (pred[144,240]{1,0:T(8,128)(4,1)S(1)}, pred[144,240]{1,0:T(8,128)(4,1)}, u32[]{:S(2)}) copy-start(pred[144,240]{1,0:T(8,128)(4,1)} %iota_compare_fusion) | copy-start | bytes 103684
  51.4 20.3 %copy-start.15 = (s32[16,15]{1,0:T(8,128)S(1)}, s32[16,15]{1,0:T(8,128)}, u32[]{:S(2)}) copy-start(s32[16,15]{1,0:T(8,128)} %multiply_add_fusion) | copy-start | bytes 2884
  51.4 20.3 %copy-start.17 = (s32[144]{0:T(256)S(1)}, s32[144]{0:T(256)}, u32[]{:S(2)}) copy-start(s32[144]{0:T(256)} %copy-done.16) | copy-start | bytes 1732
  58.5 10.6 %all-to-all-start.1 = ((f32[16,1,15]{2,1,0:T(1,128)}), f32[16,1,15]{2,1,0:T(1,128)S(1)}, u32[]{:S(2)}, u32[]{:S(2)}) async-start(f32[16,1,15]{2,1,0:T(1,128)} %copy.71), calls=%async_computation.1 | async-start | bytes 16384 | tf_op jit(solution)/shard_map/all_to_all | solution.py:241
  71.0 10.7 %copy-start.8 = (f32[1,16,9]{2,0,1:T(1,128)}, f32[1,16,9]{2,0,1:T(1,128)S(1)}, u32[]{:S(2)}) copy-start(f32[1,16,9]{2,0,1:T(1,128)S(1)} %fusion.19) | copy-start | bytes 1732
  71.1 0.5 copy-start.18
  81.7 6.9 %copy-start.6 = (bf16[768,128]{1,0:T(8,128)(2,1)S(1)}, bf16[768,128]{1,0:T(8,128)(2,1)}, u32[]{:S(2)}) copy-start(bf16[768,128]{1,0:T(8,128)(2,1)} %multiply_convert_fusion) | copy-start | bytes 589828
  86.7 1.9 %copy-start.1 = (bf16[16,3,5,32,256]{4,3,2,0,1:T(8,128)(2,1)}, bf16[16,3,5,32,256]{4,3,2,0,1:T(8,128)(2,1)S(1)}, u32[]{:S(2)}) copy-start(bf16[16,3,5,32,256]{4,3,2,0,1:T(8,128)(2,1)S(1)} %fusion.2) | copy-start | bytes 11796484
  92.5 28.5 %all-to-all-start.3 = ((bf16[16,15,4096]{2,1,0:T(8,128)(2,1)}), bf16[16,15,4096]{2,1,0:T(8,128)(2,1)S(1)}, u32[]{:S(2)}, u32[]{:S(2)}) async-start(bf16[16,15,4096]{2,1,0:T(8,128)(2,1)} %reshape.216), calls=%async_computation.3 | async-start | bytes 4194304 | tf_op jit(solution)/shard_map/all_to_all | solution.py:266
  98.4 4.4 %copy-start.10 = (f32[768]{0:T(1024)S(1)}, f32[768]{0:T(1024)}, u32[]{:S(2)}) copy-start(f32[768]{0:T(1024)} %copy-done.9) | copy-start | bytes 9220
  98.4 4.4 %copy-start.13 = (f32[768]{0:T(1024)S(1)}, f32[768]{0:T(1024)}, u32[]{:S(2)}) copy-start(f32[768]{0:T(1024)} %get-tuple-element.4) | copy-start | bytes 9220
  104.0 21.1 %copy-start.3 = (f32[512,128]{1,0:T(8,128)S(1)}, f32[512,128]{1,0:T(8,128)}, u32[]{:S(2)}) copy-start(f32[512,128]{1,0:T(8,128)} %copy-done.2) | copy-start | bytes 786436
  104.0 21.3 %copy-start.12 = (f32[512]{0:T(512)S(1)}, f32[512]{0:T(512)}, u32[]{:S(2)}) copy-start(f32[512]{0:T(512)} %copy-done.11) | copy-start | bytes 6148
  104.0 21.3 %copy-start.14 = (f32[512]{0:T(512)S(1)}, f32[512]{0:T(512)}, u32[]{:S(2)}) copy-start(f32[512]{0:T(512)} %get-tuple-element.6) | copy-start | bytes 6148
  125.1 4.5 %copy-start.4 = (f32[768,128]{1,0:T(8,128)S(1)}, f32[768,128]{1,0:T(8,128)}, u32[]{:S(2)}) copy-start(f32[768,128]{1,0:T(8,128)} %fusion.8) | copy-start | bytes 1179652
  125.6 9.1 %copy-start.5 = (f32[512,128]{1,0:T(8,128)}, f32[512,128]{1,0:T(8,128)S(1)}, u32[]{:S(2)}) copy-start(f32[512,128]{1,0:T(8,128)S(1)} %multiply_subtract_fusion) | copy-start | bytes 786436

commit v2 on v0

v2 whole, which is shorter than its diff:
```python
import functools
import jax
import jax.numpy as jnp
from jax import lax
from jax.experimental import pallas as pl
from jax.experimental.pallas import tpu as pltpu
from jax.sharding import PartitionSpec as P

MESH = pl.DeviceIdType.MESH
F32, BF16 = jnp.float32, jnp.bfloat16
SIDE = 4
sharpness_divisor = 0.1
epsilon = 1e-06
LOG2E = 1.4426950408889634


def remote(src, dst, send, recv, device):
    return pltpu.make_async_remote_copy(
        src_ref=src, dst_ref=dst, send_sem=send, recv_sem=recv, device_id=device, device_id_type=MESH
    )


def dot(a, b, ca=1, cb=0):
    return lax.dot_general(a, b, (((ca,), (cb,)), ((), ())), preferred_element_type=F32)


def inverse_norm(embedded):
    return lax.rsqrt(jnp.mean(embedded * embedded, axis=-1, keepdims=True) + epsilon)


def norm_backward(embedded, unit_grad):
    inv_norm = inverse_norm(embedded)
    inner_mean = jnp.mean(embedded * unit_grad, axis=-1, keepdims=True)
    return inv_norm * unit_grad - inv_norm * inv_norm * inv_norm * embedded * inner_mean


def pick(k, values):
    result = jnp.int32(values[0])
    for i, v in enumerate(values[1:]):
        result = jnp.where(k == i + 1, jnp.int32(v), result)
    return result


ORDER = [(0, 0), (1, 0), (3, 0), (0, 1), (0, 3), (1, 1), (1, 3), (3, 1), (3, 3),
         (2, 0), (0, 2), (2, 1), (2, 3), (1, 2), (3, 2), (2, 2)]


def kernel(n_z, qlen, cand_count,
           qh_ref, ph_ref, proj_ref, cand_ref,
           loss_ref, qg_ref, pg_ref, wg_ref,
           qh, ph, qe, pe, pt, pone, gq, ex, gn, qn, acc, cbuf, mask, mark, score, gsrep,
           sbuf1, sbuf2, rbuf1, rbuf2, sum1, gp, qgb, pgb,
           wg, out, half, got0, part, got1, mine, got2,
           sem_h, c_s, c_r, sc_s, sc_r, a_s, a_r, b_s, b_r,
           s0, r0, s1, r1, s2, r2, s3, r3, s4, r4, s5, r5):
    n_pa = SIDE * SIDE
    rows_q = qh.shape[0]
    hrow = rows_q // 2
    qrow = hrow // 2
    queries = rows_q // qlen
    n_p, plen = pone.shape[0], pone.shape[1]
    width = qh.shape[1]
    vec = proj_ref.shape[1]
    me, pb = lax.axis_index("pa"), lax.axis_index("pb")
    y, x = me // SIDE, me % SIDE
    z, core = pb // 2, pb % 2
    partner = {"pb": z * 2 + (1 - core)}
    scale = 1.0 / (vec * sharpness_divisor)

    def xy(k):
        return lax.rem(me + k, n_pa)

    def zz(k):
        return lax.rem(z + k, n_z)

    def load_q(k):
        at = pl.ds(k * hrow, hrow)
        return pltpu.make_async_copy(qh_ref.at[at], qh.at[at], sem_h.at[k])

    def load_p(k):
        at = pl.ds(k * plen, plen)
        return pltpu.make_async_copy(ph_ref.at[at], ph.at[at], sem_h.at[2 + k])

    for k in range(2):
        load_q(k).start()
    for k in range(n_p):
        load_p(k).start()

    barrier = pltpu.get_barrier_semaphore()
    pl.semaphore_signal(barrier, inc=1, device_id=partner, device_id_type=MESH)

    @pl.loop(1, n_pa)
    def _(k):
        pl.semaphore_signal(barrier, inc=1, device_id={"pa": xy(k)}, device_id_type=MESH)

    @pl.loop(1, n_z)
    def _(k):
        pl.semaphore_signal(barrier, inc=1, device_id={"pb": zz(k) * 2 + core}, device_id_type=MESH)

    lane = lax.broadcasted_iota(jnp.int32, (128, 128), 1)
    line = lax.broadcasted_iota(jnp.int32, (128, 128), 0)
    place = (lane == line + (me % 8) * queries).astype(F32) * (line < queries).astype(F32)
    cbuf[me] = dot(cand_ref[...], place)
    score[...] = jnp.zeros_like(score)
    acc[...] = jnp.zeros_like(acc)

    def slot(h, d1, d2):
        dx, dy = d1 * (1 - h) + d2 * h, d2 * (1 - h) + d1 * h
        return lax.rem(y + dy, SIDE) * SIDE + lax.rem(x + dx, SIDE)

    def offset(h, g, o):
        first = jnp.int32(g == 0) if isinstance(g, int) else (g == 0).astype(jnp.int32)
        d1 = first * o + (1 - first) * (g - 1)
        return d1, (1 - first) * o

    def neighbour(h, g, o):
        first = jnp.int32(g == 0) if isinstance(g, int) else (g == 0).astype(jnp.int32)
        return {"pa": slot(h, first * o, (1 - first) * o)}

    def whole(h, g, o, k, to):
        block = gq.at[slot(h, *offset(h, g, o)), pl.ds(h * hrow, hrow)]
        i = (h * 5 + g) * 4 + k
        return remote(block, block, a_s.at[i], a_r.at[i], neighbour(h, g, to))

    def quarter(h, g, o, k, to):
        block = gq.at[slot(h, *offset(h, g, o)), pl.ds(h * hrow + (k - 2) * qrow, qrow)]
        i = (h * 5 + g) * 4 + k
        return remote(block, block, a_s.at[i], a_r.at[i], neighbour(h, g, to))

    def send_whole(h, g):
        whole(h, g, 0, 0, 1).start()
        whole(h, g, 0, 1, 3).start()

    def pass_on(h, g):
        whole(h, g, 3, 0, 1).wait_recv()
        quarter(h, g, 3, 2, 1).start()
        whole(h, g, 1, 1, 3).wait_recv()
        quarter(h, g, 1, 3, 3).start()

    def finish(h, g):
        quarter(h, g, 2, 2, 1).wait_recv()
        quarter(h, g, 2, 3, 3).wait_recv()

    def sent(h, g):
        whole(h, g, 0, 0, 1).wait_send()
        whole(h, g, 0, 1, 3).wait_send()
        quarter(h, g, 3, 2, 1).wait_send()
        quarter(h, g, 1, 3, 3).wait_send()

    def to_all(buf, send, recv, k):
        return remote(buf.at[me], buf.at[me], send.at[k], recv.at[n_pa - k], {"pa": xy(k)})

    def from_all(buf, send, recv, k):
        return remote(buf.at[xy(k)], buf.at[xy(k)], send.at[k], recv.at[k], {"pa": xy(k)})

    for h in range(2):
        at = pl.ds(h * hrow, hrow)
        load_q(h).wait()
        e = dot(qh[at, :], proj_ref[...])
        qe[at, :] = e
        gq[me, at, :] = (e * inverse_norm(e)).astype(BF16)
        if h == 0:
            pl.semaphore_wait(barrier, n_pa + n_z - 1)
        send_whole(h, 0)
        send_whole(h, 1)

    @pl.loop(1, n_pa)
    def _(k):
        to_all(cbuf, c_s, c_r, k).start()

    def project_passage(k):
        load_p(k).wait()
        at = pl.ds(k * plen, plen)
        e = dot(ph[at, :], proj_ref[...])
        pe[at, :] = e
        u = (e * inverse_norm(e)).astype(BF16)
        pone[k, :, 0:vec] = u
        pone[k, :, vec:] = jnp.ones((plen, vec), BF16)
        pt[k] = u.astype(F32).T.astype(BF16)

    project_passage(0)

    @pl.loop(0, 2)
    def _(h):
        pass_on(h, 0)
        send_whole(h, 2)
        send_whole(h, 4)

    project_passage(1)

    @pl.loop(0, 2)
    def _(h):
        pass_on(h, 1)

    for k in range(2, n_p):
        project_passage(k)

    @pl.loop(0, 2)
    def _(h):
        finish(h, 0)
        send_whole(h, 3)

    narrow = lax.broadcasted_iota(jnp.int32, (8, 128), 1)

    @pl.loop(0, n_pa)
    def _(k):
        @pl.when(k == 1)
        def _():
            @pl.loop(0, 2)
            def _(h):
                pass_on(h, 2)
                pass_on(h, 4)

        @pl.when(k == 6)
        def _():
            @pl.loop(0, 2)
            def _(h):
                pass_on(h, 3)

        @pl.when(k == 9)
        def _():
            @pl.loop(0, 2)
            def _(h):
                finish(h, 1)

        @pl.when(k == 11)
        def _():
            @pl.loop(0, 2)
            def _(h):
                finish(h, 2)
                finish(h, 4)

        @pl.when(k == 15)
        def _():
            @pl.loop(0, 2)
            def _(h):
                finish(h, 3)

        dx, dy = pick(k, [d[0] for d in ORDER]), pick(k, [d[1] for d in ORDER])
        b = lax.rem(y + dy, SIDE) * SIDE + lax.rem(x + dx, SIDE)
        u = gq[b]
        at = pl.ds(pl.multiple_of(b * rows_q, rows_q), rows_q)
        for p in range(n_p):
            e = jnp.exp2(dot(u, pt[p]) * (LOG2E * scale)).astype(BF16)
            ex[p, at, :] = e
            sums = dot(e, pone[p])
            total = sums[:, vec:]
            inverse = 1.0 / total
            gn[p, at, :] = (sums[:, :vec] * inverse).astype(BF16)
            qn[p, at, :] = (u.astype(F32) * inverse).astype(BF16)
            four = total.reshape(queries, 4, qlen // 4, vec)
            logs = jnp.log((four[:, 0] * four[:, 1]) * (four[:, 2] * four[:, 3]))
            s = acc[p, b // 8]
            for i in range(queries):
                s = s + jnp.where(narrow == lax.rem(b, 8) * queries + i, logs[i], 0.0)
            acc[p, b // 8] = s

    for p in range(n_p):
        for i in range(2):
            score[me, p:p + 1, i * 128:(i + 1) * 128] = sharpness_divisor * jnp.sum(acc[p, i], axis=0, keepdims=True)

    @pl.loop(1, n_pa)
    def _(k):
        to_all(score, sc_s, sc_r, k).start()

    @pl.loop(1, n_pa)
    def _(k):
        from_all(cbuf, c_s, c_r, k).wait_recv()

    left, right = cbuf[0], cbuf[8]
    for i in range(1, 8):
        left = left + cbuf[i]
        right = right + cbuf[8 + i]
    named = jnp.concatenate([left, right], axis=1).astype(jnp.int32)
    rank = lax.broadcasted_iota(jnp.int32, (8, 256), 0)

    @pl.loop(0, n_pa)
    def _(o):
        ident = jnp.where(rank < n_p, o * n_p + rank, -1)
        first = (named[0:1, :] == ident).astype(F32)
        found = first
        for c in range(1, cand_count):
            found = found + (named[c:c + 1, :] == ident).astype(F32)
        mask[o] = found
        mark[o] = first

    @pl.loop(1, n_pa)
    def _(k):
        from_all(score, sc_s, sc_r, k).wait_recv()

    similarity = score[...]
    exponent = jnp.exp(similarity) * mask[...]
    element_total = jnp.sum(jnp.sum(exponent, axis=0), axis=0, keepdims=True)
    chosen = jnp.sum(jnp.sum(similarity * mark[...], axis=0), axis=0, keepdims=True)
    loss = jnp.log(element_total) - chosen
    mine_row = lax.broadcasted_iota(jnp.int32, (queries, 256), 1) == lax.broadcasted_iota(
        jnp.int32, (queries, 256), 0) + me * queries
    loss_ref[...] = jnp.broadcast_to(
        jnp.sum(jnp.where(mine_row, loss, 0.0), axis=1, keepdims=True), loss_ref.shape)
    grad_score = (jnp.exp(score[me]) * mask[me] / element_total - mark[me]) * (1.0 / vec)
    for p in range(n_p):
        gsrep[p] = jnp.broadcast_to(grad_score[p:p + 1, :], (vec, 256)).T

    q_half = queries // 2

    def spread(p, b, h, count):
        g = gsrep[p, pl.ds(pl.multiple_of(b * queries + h * q_half, 8), count), :]
        return jnp.broadcast_to(g[:, None, :], (count, qlen, vec)).reshape(count * qlen, vec)

    def value(h, g, o):
        if isinstance(g, int) and g == 0:
            return sum1[h * SIDE + o]
        b = slot(h, g - 1, o)
        at = pl.ds(pl.multiple_of(b * rows_q + h * hrow, hrow), hrow)
        result = spread(0, b, h, q_half) * gn[0, at, :].astype(F32)
        for p in range(1, n_p):
            result = result + spread(p, b, h, q_half) * gn[p, at, :].astype(F32)
        return result

    def leg1(h, g, k, to):
        i = h * 5 + g
        at = pl.ds(k * qrow, qrow)
        return remote(sbuf1.at[i, at], rbuf1.at[i, at], b_s.at[i * 4 + k], b_r.at[i * 4 + k], neighbour(h, g, to))

    def leg2(h, g, k, to):
        i = h * 5 + g
        return remote(sbuf2.at[i * 2 + k], rbuf2.at[i * 2 + k], b_s.at[i * 4 + 2 + k], b_r.at[i * 4 + 2 + k],
                      neighbour(h, g, to))

    def step1(h, g):
        sbuf1[h * 5 + g] = value(h, g, 2).astype(BF16)
        leg1(h, g, 0, 1).start()
        leg1(h, g, 1, 3).start()

    def step2(h, g):
        i = h * 5 + g
        v = value(h, g, 1)
        leg1(h, g, 0, 1).wait_recv()
        sbuf2[i * 2, 0:qrow, :] = (v[0:qrow] + rbuf1[i, 0:qrow, :].astype(F32)).astype(BF16)
        sbuf2[i * 2, qrow:, :] = v[qrow:].astype(BF16)
        leg2(h, g, 0, 1).start()
        v = value(h, g, 3)
        leg1(h, g, 1, 3).wait_recv()
        sbuf2[i * 2 + 1, 0:qrow, :] = v[0:qrow].astype(BF16)
        sbuf2[i * 2 + 1, qrow:, :] = (v[qrow:] + rbuf1[i, qrow:, :].astype(F32)).astype(BF16)
        leg2(h, g, 1, 3).start()

    def step3(h, g):
        i = h * 5 + g
        v = value(h, g, 0)
        leg2(h, g, 0, 1).wait_recv()
        v = v + rbuf2[i * 2].astype(F32)
        leg2(h, g, 1, 3).wait_recv()
        return v + rbuf2[i * 2 + 1].astype(F32)

    def grad_passage(first, last):
        @pl.loop(first, last)
        def _(b):
            at = pl.ds(pl.multiple_of(b * rows_q, rows_q), rows_q)
            for p in range(n_p):
                w = (spread(p, b, 0, queries) * qn[p, at, :].astype(F32)).astype(BF16)
                gp[p] += dot(ex[p, at, :], w, 0, 0)

    gp[...] = jnp.zeros_like(gp)

    @pl.loop(0, 8)
    def _(i):
        step1(i % 2, 1 + lax.rem(i // 2 + 2, SIDE))

    grad_passage(0, 3)

    @pl.loop(0, 8)
    def _(i):
        step2(i % 2, 1 + lax.rem(i // 2 + 2, SIDE))

    grad_passage(3, 9)

    @pl.loop(0, 2)
    def _(h):
        sum1[h * SIDE + 2] = step3(h, 3)
        step1(h, 0)

    grad_passage(9, 12)

    @pl.loop(0, 2)
    def _(h):
        sum1[h * SIDE + 1] = step3(h, 2)
        sum1[h * SIDE + 3] = step3(h, 4)
        sum1[h * SIDE] = step3(h, 1)
        step2(h, 0)

    grad_passage(12, 16)

    for p in range(n_p):
        at = pl.ds(p * plen, plen)
        g = norm_backward(pe[at, :], gp[p])
        pg_ref[at, :] = g
        pgb[at, :] = g.astype(BF16)

    quarter_rows = width // 8

    @pl.loop(0, 8)
    def _(c):
        at = pl.ds(pl.multiple_of(c * quarter_rows, quarter_rows), quarter_rows)
        wg[at, :] = dot(ph[:, at], pgb[...], 0, 0)

    for h in range(2):
        at = pl.ds(h * hrow, hrow)
        g = norm_backward(qe[at, :], step3(h, 0))
        qg_ref[at, :] = g
        qgb[at, :] = g.astype(BF16)

    half_rows = width // 2
    chunk = half_rows // n_pa
    piece = chunk // n_z
    base = core * half_rows

    def swap(j):
        at = pl.ds(pl.multiple_of(lax.rem(y + 1 + j, SIDE) * quarter_rows, quarter_rows), quarter_rows)
        return remote(half.at[at], got0.at[at], s0.at[j], r0.at[j], partner)

    def product(first, j):
        at = pl.ds(pl.multiple_of(first + lax.rem(y + 1 + j, SIDE) * quarter_rows, quarter_rows), quarter_rows)
        return wg[at, :] + dot(qh[:, at], qgb[...], 0, 0)

    @pl.loop(0, SIDE)
    def _(j):
        at = pl.ds(pl.multiple_of(lax.rem(y + 1 + j, SIDE) * quarter_rows, quarter_rows), quarter_rows)
        half[at, :] = product(half_rows - base, j).astype(BF16)
        swap(j).start()

    def to_xy(k, peer):
        return remote(part.at[peer], got1.at[me], s1.at[k], r1.at[n_pa - k], {"pa": peer})

    @pl.loop(0, SIDE)
    def _(j):
        v = product(base, j)
        row = lax.rem(y + 1 + j, SIDE)
        swap(j).wait_recv()
        v = v + got0[pl.ds(pl.multiple_of(row * quarter_rows, quarter_rows), quarter_rows), :].astype(F32)
        for i in range(SIDE):
            part[row * SIDE + i] = v[i * chunk:(i + 1) * chunk].astype(BF16)

            @pl.when((row == y) & (x == i))
            def _():
                mine[...] = v[i * chunk:(i + 1) * chunk]

        @pl.loop(1, SIDE + 1)
        def _(i):
            peer = row * SIDE + lax.rem(x + i, SIDE)

            @pl.when(peer != me)
            def _():
                to_xy(lax.rem(peer + n_pa - me, n_pa), peer).start()

    @pl.loop(1, n_pa)
    def _(k):
        remote(part.at[xy(k)], got1.at[xy(k)], s1.at[k], r1.at[k], {"pa": xy(k)}).wait_recv()
        mine[...] += got1[xy(k)].astype(F32)

    part[me] = mine[...].astype(BF16)

    def to_z(k):
        return remote(part.at[me, pl.ds(zz(k) * piece, piece)], got2.at[z], s2.at[k],
                      r2.at[n_z - k], {"pb": zz(k) * 2 + core})

    @pl.loop(1, n_z)
    def _(k):
        to_z(k).start()

    total = mine[pl.ds(z * piece, piece), :]
    for k in range(1, n_z):
        remote(got2.at[zz(k)], got2.at[zz(k)], s2.at[k], r2.at[k], {"pb": zz(k) * 2 + core}).wait_recv()
        total = total + got2[zz(k)].astype(F32)

    out[pl.ds(base + me * chunk + z * piece, piece), :] = total.astype(BF16)

    def back_z(k, who, recv):
        at = pl.ds(base + me * chunk + who * piece, piece)
        return remote(out.at[at], out.at[at], s3.at[k], r3.at[recv], {"pb": zz(k) * 2 + core})

    @pl.loop(1, n_z)
    def _(k):
        back_z(k, z, n_z - k).start()

    @pl.loop(1, n_z)
    def _(k):
        back_z(k, zz(k), k).wait_recv()

    def back_xy(k, who, recv):
        at = pl.ds(base + who * chunk, chunk)
        return remote(out.at[at], out.at[at], s4.at[k], r4.at[recv], {"pa": xy(k)})

    @pl.loop(1, n_pa)
    def _(k):
        back_xy(k, me, n_pa - k).start()

    def across(k, first):
        at = pl.ds(first + xy(k) * chunk, chunk)
        return remote(out.at[at], out.at[at], s5.at[k], r5.at[k], partner)

    across(0, base).start()

    @pl.loop(1, n_pa)
    def _(k):
        back_xy(k, xy(k), k).wait_recv()
        across(k, base).start()

    @pl.loop(0, n_pa)
    def _(k):
        across(k, half_rows - base).wait_recv()

    wg_ref[...] = out[...]

    @pl.loop(0, 10)
    def _(i):
        h, g = i // 5, lax.rem(i, 5)
        sent(h, g)
        leg1(h, g, 0, 1).wait_send()
        leg1(h, g, 1, 3).wait_send()
        leg2(h, g, 0, 1).wait_send()
        leg2(h, g, 1, 3).wait_send()

    @pl.loop(1, n_pa)
    def _(k):
        to_all(cbuf, c_s, c_r, k).wait_send()
        to_all(score, sc_s, sc_r, k).wait_send()
        to_xy(k, xy(k)).wait_send()
        back_xy(k, me, n_pa - k).wait_send()

    @pl.loop(1, n_z)
    def _(k):
        to_z(k).wait_send()
        back_z(k, z, n_z - k).wait_send()

    @pl.loop(0, SIDE)
    def _(j):
        swap(j).wait_send()

    @pl.loop(0, n_pa)
    def _(k):
        across(k, base).wait_send()


def shards(query_hidden, passage_hidden, projection, candidates):
    queries, qlen, width = query_hidden.shape
    n_p, plen, _ = passage_hidden.shape
    vec = projection.shape[1]
    n_pa, n_z = lax.axis_size("pa"), lax.axis_size("pb") // 2
    rows_q, rows_p = queries * qlen, n_p * plen
    all_rows = n_pa * rows_q
    hrow = rows_q // 2
    half_rows = width // 2
    chunk = half_rows // n_pa
    piece = chunk // n_z
    cand = jnp.pad(candidates.T.astype(F32), ((0, 16 - candidates.shape[1]), (0, 128 - queries)))
    dma = pltpu.SemaphoreType.DMA
    V = pltpu.VMEM
    in_vmem, anywhere = pl.BlockSpec(memory_space=pltpu.VMEM), pl.BlockSpec(memory_space=pl.ANY)
    loss, query_grad, passage_grad, weight_grad = pl.pallas_call(
        functools.partial(kernel, n_z, qlen, candidates.shape[1]),
        out_shape=(
            jax.ShapeDtypeStruct((queries, 128), F32),
            jax.ShapeDtypeStruct((rows_q, vec), F32),
            jax.ShapeDtypeStruct((rows_p, vec), F32),
            jax.ShapeDtypeStruct((width, vec), BF16),
        ),
        in_specs=[anywhere, anywhere, in_vmem, in_vmem],
        out_specs=(in_vmem,) * 4,
        scratch_shapes=[
            V((rows_q, width), BF16), V((rows_p, width), BF16), V((rows_q, vec), F32), V((rows_p, vec), F32),
            V((n_p, vec, plen), BF16), V((n_p, plen, 2 * vec), BF16), V((n_pa, rows_q, vec), BF16),
            V((n_p, all_rows, plen), BF16), V((n_p, all_rows, vec), BF16), V((n_p, all_rows, vec), BF16),
            V((n_p, 2, 8, 128), F32), V((n_pa, 16, 128), F32), V((n_pa, 8, 256), F32), V((n_pa, 8, 256), F32),
            V((n_pa, 8, 256), F32), V((n_p, 256, vec), F32),
            V((10, hrow, vec), BF16), V((20, hrow, vec), BF16), V((10, hrow, vec), BF16), V((20, hrow, vec), BF16),
            V((2 * SIDE, hrow, vec), F32), V((n_p, plen, vec), F32), V((rows_q, vec), BF16), V((rows_p, vec), BF16),
            V((width, vec), F32), V((width, vec), BF16), V((half_rows, vec), BF16), V((half_rows, vec), BF16),
            V((n_pa, chunk, vec), BF16), V((n_pa, chunk, vec), BF16), V((chunk, vec), F32), V((n_z, piece, vec), BF16),
            dma((2 + n_p,)), dma((n_pa,)), dma((n_pa,)), dma((n_pa,)), dma((n_pa,)),
            dma((40,)), dma((40,)), dma((40,)), dma((40,)),
            dma((SIDE,)), dma((SIDE,)), dma((n_pa,)), dma((n_pa,)), dma((n_z,)), dma((n_z,)),
            dma((n_z,)), dma((n_z,)), dma((n_pa,)), dma((n_pa,)), dma((n_pa,)), dma((n_pa,)),
        ],
        compiler_params=pltpu.CompilerParams(collective_id=0, has_side_effects=True, vmem_limit_bytes=60 * 2**20),
        name="retriever",
    )(query_hidden.reshape(rows_q, width), passage_hidden.reshape(rows_p, width), projection, cand)
    return (
        loss[:, 0],
        query_grad.reshape(queries, qlen, vec),
        passage_grad.reshape(n_p, plen, vec),
        weight_grad.astype(F32),
    )


def solution(mesh):
    placed = (P(("pb", "pa"), None, None), P(("pb", "pa"), None, None), P(), P(("pb", "pa"), None))
    return jax.shard_map(
        shards,
        mesh=mesh,
        in_specs=placed,
        out_specs=(P(("pb", "pa")), P(("pb", "pa"), None, None), P(("pb", "pa"), None, None), P()),
        check_vma=False,
    )
```

time: 420 us -> 101 us (0.24)
  waiting for transfers between devices: 312 us -> 0 us
  Pallas kernels: 0 us -> 91.1 us
  matrix products: 28.7 us -> 0 us
  starting transfers between devices: 16.5 us -> 0 us
  local copies, waits for them, and re-layouts: 22.3 us -> 6.14 us
  between operations: 14.4 us -> 0.64 us
  other arithmetic: 15.7 us -> 2.68 us
  blocking collectives: 9.11 us -> 0 us
    psum x1 -> x0, waiting for transfers between devices: 263 us -> none  [shards(): weight_grad = lax.psum(local_sum, ('pb', 'pa'))]
    pallas_call x0 -> x1, Pallas kernels: none -> 91.1 us  [shards(): pl.pallas_call(functools.partial(kernel, n_z, qlen, candidates.shape[1]),...]
    all_to_all x3 -> x0, waiting for transfers between devices: 49 us -> none  [the longest x1 23.1 us: shards(): lax.all_to_all(outgoing, 'pa', split_axis=0, concat_axis=0, tiled=True)]
    dot_general x11 -> x0, matrix products: 28.7 us -> none  [the longest x2 8.17 us: project_rows(): jnp.dot(flattened, projection, preferred_element_type=jnp.float32)]
    all_to_all x3 -> x0, starting transfers between devices: 16.3 us -> none  [the longest x1 7.58 us: shards(): lax.all_to_all(outgoing, 'pa', split_axis=0, concat_axis=0, tiled=True)]
    all_to_all x1 -> x0, blocking collectives: 9.11 us -> none  [shards(): lax.all_to_all(slot_grad.reshape(shard_count, passage_count * slot_most),...]
    reshape x7 -> x0, local copies, waits for them, and re-layouts: 8.28 us -> none  [the longest x1 2.97 us: shards(): returned_grads.reshape(slot_count, query_len * vector_dimension)]
    convert_element_type x2 -> x0, local copies, waits for them, and re-layouts: 5.97 us -> none  [shards(): returned_grads = lax.all_to_all(slot_query.reshape(shard_count, passage_c...]
  transfers between devices with their start and end apart: 4 -> 0, of which waited for: 4 -> 0; matrix products, arithmetic and copies ran while one was open for 3% -> 0% of each run, Pallas kernels for 0% -> 0%
where the time goes in v2:
time: 101 us
  Pallas kernels  91.1 us (90%)
  local copies, waits for them, and re-layouts  6.14 us (6%)
  other arithmetic  2.68 us (3%)
    pallas_call x1, Pallas kernels, shards(): pl.pallas_call(functools.partial(kernel, n_z, qlen, candidates.shape[1]),...  91.1 us
    unnamed x3, local copies, waits for them, and re-layouts  4.21 us
    convert_element_type x1, other arithmetic, shards(): weight_grad.astype(F32)  2.68 us

profile of v2, /device:TPU:1, one launch (start us, length us, event | category | flops | bytes accessed | tf_op | source)
XLA Modules:
  0.0 100.5 jit_solution(12249543138755706569)
XLA Ops:
  0.6 0.8 copy.9
  1.4 0.6 pad.4.cand_ref
  2.0 91.1 %retriever.1 = (f32[16,128]{1,0:T(8,128)}, f32[512,128]{1,0:T(8,128)}, f32[768,128]{1,0:T(8,128)}, bf16[4096,128]{1,0:T(8,128)(2,1)}) custom-call(bf16[512,4096]{1,0:T(8,128)(2,1)} %bitcast.7, bf16[768,4096]{1,0:T(8,128)(2,1)} %bitcast.6, bf16[4096,128]{1,0:T(8,128)(2,1)} %proj_ref.1, f32[16,128]{1,0:T(8,128)} %pad.4.cand_ref), custom_call_target="tpu_custom_call" | custom-call | tf_op jit(solution)/shard_map/retriever/pallas_call | solution.py:560
  93.1 1.3 %slice_reduce_fusion = f32[16]{0:T(128)} fusion(f32[16,128]{1,0:T(8,128)} %get-tuple-element.8), kind=kLoop, calls=%fused_computation | loop fusion | bytes 128 | tf_op jit(solution)/shard_map/slice | solution.py:589
  94.4 2.7 %convert_element_type.13 = f32[4096,128]{1,0:T(8,128)} convert(bf16[4096,128]{1,0:T(8,128)(2,1)} %get-tuple-element.11) | non-fusion elementwise | flops 524288 | bytes 3145728 | tf_op jit(solution)/shard_map/convert_element_type | solution.py:592
  97.1 1.7 %copy.12 = f32[16,32,128]{2,1,0:T(8,128)} copy(f32[16,32,128]{2,1,0:T(8,128)} %bitcast.9) | data formatting | bytes 524288
  98.8 1.8 %copy.13 = f32[3,256,128]{2,1,0:T(8,128)} copy(f32[3,256,128]{2,1,0:T(8,128)} %bitcast.8) | data formatting | bytes 786432
  (1 shorter events, 0.0 us)

commit v3 on v2

--- a/solution.py
+++ b/solution.py
@@ -52,7 +52,7 @@
            sbuf1, sbuf2, rbuf1, rbuf2, sum1, gp, qgb, pgb,
            wg, out, half, got0, part, got1, mine, got2,
            sem_h, c_s, c_r, sc_s, sc_r, a_s, a_r, b_s, b_r,
-           s0, r0, s1, r1, s2, r2, s3, r3, s4, r4, s5, r5):
+           s0, r0, s1, r1, s2, r2, s4, r4, s5, r5):
     n_pa = SIDE * SIDE
     rows_q = qh.shape[0]
     hrow = rows_q // 2
@@ -97,10 +97,11 @@
     def _(k):
         pl.semaphore_signal(barrier, inc=1, device_id={"pb": zz(k) * 2 + core}, device_id_type=MESH)
 
-    lane = lax.broadcasted_iota(jnp.int32, (128, 128), 1)
-    line = lax.broadcasted_iota(jnp.int32, (128, 128), 0)
-    place = (lane == line + (me % 8) * queries).astype(F32) * (line < queries).astype(F32)
-    cbuf[me] = dot(cand_ref[...], place)
+    lane = lax.broadcasted_iota(jnp.int32, (queries, 128), 1)
+    line = lax.broadcasted_iota(jnp.int32, (queries, 128), 0)
+    place = (lane == line + (me % 8) * queries).astype(F32)
+    cbuf[me] = jnp.zeros((16, 128), F32)
+    cbuf[me, 0:cand_count, :] = dot(cand_ref[...].astype(F32), place, 0, 0)
     score[...] = jnp.zeros_like(score)
     acc[...] = jnp.zeros_like(acc)
 
@@ -195,23 +196,25 @@
     for k in range(2, n_p):
         project_passage(k)
 
-    @pl.loop(0, 2)
-    def _(h):
-        finish(h, 0)
-        send_whole(h, 3)
-
     narrow = lax.broadcasted_iota(jnp.int32, (8, 128), 1)
 
     @pl.loop(0, n_pa)
     def _(k):
-        @pl.when(k == 1)
+        @pl.when(k == 2)
+        def _():
+            @pl.loop(0, 2)
+            def _(h):
+                finish(h, 0)
+                send_whole(h, 3)
+
+        @pl.when(k == 4)
         def _():
             @pl.loop(0, 2)
             def _(h):
                 pass_on(h, 2)
                 pass_on(h, 4)
 
-        @pl.when(k == 6)
+        @pl.when(k == 7)
         def _():
             @pl.loop(0, 2)
             def _(h):
@@ -295,8 +298,8 @@
     loss = jnp.log(element_total) - chosen
     mine_row = lax.broadcasted_iota(jnp.int32, (queries, 256), 1) == lax.broadcasted_iota(
         jnp.int32, (queries, 256), 0) + me * queries
-    loss_ref[...] = jnp.broadcast_to(
-        jnp.sum(jnp.where(mine_row, loss, 0.0), axis=1, keepdims=True), loss_ref.shape)
+    column = jnp.sum(jnp.where(mine_row, loss, 0.0), axis=1, keepdims=True)
+    loss_ref[...] = jnp.sum(jnp.where(lane == line, column, 0.0), axis=0, keepdims=True)
     grad_score = (jnp.exp(score[me]) * mask[me] / element_total - mark[me]) * (1.0 / vec)
     for p in range(n_p):
         gsrep[p] = jnp.broadcast_to(grad_score[p:p + 1, :], (vec, 256)).T
@@ -412,7 +415,6 @@
 
     half_rows = width // 2
     chunk = half_rows // n_pa
-    piece = chunk // n_z
     base = core * half_rows
 
     def swap(j):
@@ -459,33 +461,23 @@
         mine[...] += got1[xy(k)].astype(F32)
 
     part[me] = mine[...].astype(BF16)
-
-    def to_z(k):
-        return remote(part.at[me, pl.ds(zz(k) * piece, piece)], got2.at[z], s2.at[k],
-                      r2.at[n_z - k], {"pb": zz(k) * 2 + core})
+    got2[z] = mine[...].astype(BF16)
+
+    def to_z(k, who, recv):
+        return remote(part.at[me], got2.at[who], s2.at[k], r2.at[recv], {"pb": zz(k) * 2 + core})
 
     @pl.loop(1, n_z)
     def _(k):
-        to_z(k).start()
-
-    total = mine[pl.ds(z * piece, piece), :]
+        to_z(k, z, n_z - k).start()
+
+    @pl.loop(1, n_z)
+    def _(k):
+        to_z(k, zz(k), k).wait_recv()
+
+    total = got2[0].astype(F32)
     for k in range(1, n_z):
-        remote(got2.at[zz(k)], got2.at[zz(k)], s2.at[k], r2.at[k], {"pb": zz(k) * 2 + core}).wait_recv()
-        total = total + got2[zz(k)].astype(F32)
-
-    out[pl.ds(base + me * chunk + z * piece, piece), :] = total.astype(BF16)
-
-    def back_z(k, who, recv):
-        at = pl.ds(base + me * chunk + who * piece, piece)
-        return remote(out.at[at], out.at[at], s3.at[k], r3.at[recv], {"pb": zz(k) * 2 + core})
-
-    @pl.loop(1, n_z)
-    def _(k):
-        back_z(k, z, n_z - k).start()
-
-    @pl.loop(1, n_z)
-    def _(k):
-        back_z(k, zz(k), k).wait_recv()
+        total = total + got2[k].astype(F32)
+    out[pl.ds(base + me * chunk, chunk), :] = total.astype(BF16)
 
     def back_xy(k, who, recv):
         at = pl.ds(base + who * chunk, chunk)
@@ -530,8 +522,7 @@
 
     @pl.loop(1, n_z)
     def _(k):
-        to_z(k).wait_send()
-        back_z(k, z, n_z - k).wait_send()
+        to_z(k, z, n_z - k).wait_send()
 
     @pl.loop(0, SIDE)
     def _(j):
@@ -540,6 +531,13 @@
     @pl.loop(0, n_pa)
     def _(k):
         across(k, base).wait_send()
+
+
+def hand_over(loss_ref, qg_ref, pg_ref, wg_ref, loss_out, qg_out, pg_out, wg_out):
+    loss_out[...] = loss_ref[:, 0:loss_out.shape[1]]
+    qg_out[...] = qg_ref[...]
+    pg_out[...] = pg_ref[...]
+    wg_out[...] = wg_ref[...].astype(F32)
 
 
 def shards(query_hidden, passage_hidden, projection, candidates):
@@ -552,15 +550,13 @@
     hrow = rows_q // 2
     half_rows = width // 2
     chunk = half_rows // n_pa
-    piece = chunk // n_z
-    cand = jnp.pad(candidates.T.astype(F32), ((0, 16 - candidates.shape[1]), (0, 128 - queries)))
     dma = pltpu.SemaphoreType.DMA
     V = pltpu.VMEM
     in_vmem, anywhere = pl.BlockSpec(memory_space=pltpu.VMEM), pl.BlockSpec(memory_space=pl.ANY)
     loss, query_grad, passage_grad, weight_grad = pl.pallas_call(
         functools.partial(kernel, n_z, qlen, candidates.shape[1]),
         out_shape=(
-            jax.ShapeDtypeStruct((queries, 128), F32),
+            jax.ShapeDtypeStruct((1, 128), F32),
             jax.ShapeDtypeStruct((rows_q, vec), F32),
             jax.ShapeDtypeStruct((rows_p, vec), F32),
             jax.ShapeDtypeStruct((width, vec), BF16),
@@ -576,20 +572,32 @@
             V((10, hrow, vec), BF16), V((20, hrow, vec), BF16), V((10, hrow, vec), BF16), V((20, hrow, vec), BF16),
             V((2 * SIDE, hrow, vec), F32), V((n_p, plen, vec), F32), V((rows_q, vec), BF16), V((rows_p, vec), BF16),
             V((width, vec), F32), V((width, vec), BF16), V((half_rows, vec), BF16), V((half_rows, vec), BF16),
-            V((n_pa, chunk, vec), BF16), V((n_pa, chunk, vec), BF16), V((chunk, vec), F32), V((n_z, piece, vec), BF16),
+            V((n_pa, chunk, vec), BF16), V((n_pa, chunk, vec), BF16), V((chunk, vec), F32), V((n_z, chunk, vec), BF16),
             dma((2 + n_p,)), dma((n_pa,)), dma((n_pa,)), dma((n_pa,)), dma((n_pa,)),
             dma((40,)), dma((40,)), dma((40,)), dma((40,)),
             dma((SIDE,)), dma((SIDE,)), dma((n_pa,)), dma((n_pa,)), dma((n_z,)), dma((n_z,)),
-            dma((n_z,)), dma((n_z,)), dma((n_pa,)), dma((n_pa,)), dma((n_pa,)), dma((n_pa,)),
+            dma((n_pa,)), dma((n_pa,)), dma((n_pa,)), dma((n_pa,)),
         ],
         compiler_params=pltpu.CompilerParams(collective_id=0, has_side_effects=True, vmem_limit_bytes=60 * 2**20),
         name="retriever",
-    )(query_hidden.reshape(rows_q, width), passage_hidden.reshape(rows_p, width), projection, cand)
+    )(query_hidden.reshape(rows_q, width), passage_hidden.reshape(rows_p, width), projection, candidates)
+    loss, query_grad, passage_grad, weight_grad = pl.pallas_call(
+        hand_over,
+        out_shape=(
+            jax.ShapeDtypeStruct((1, queries), F32),
+            jax.ShapeDtypeStruct((rows_q, vec), F32),
+            jax.ShapeDtypeStruct((rows_p, vec), F32),
+            jax.ShapeDtypeStruct((width, vec), F32),
+        ),
+        in_specs=[in_vmem] * 4,
+        out_specs=(in_vmem,) * 4,
+        name="hand_over",
+    )(loss, query_grad, passage_grad, weight_grad)
     return (
-        loss[:, 0],
+        loss.reshape(queries),
         query_grad.reshape(queries, qlen, vec),
         passage_grad.reshape(n_p, plen, vec),
-        weight_grad.astype(F32),
+        weight_grad,
     )
 
 

time: 101 us -> 92.5 us (0.916)
  local copies, waits for them, and re-layouts: 6.14 us -> 0 us
  other arithmetic: 2.68 us -> 0 us
    unnamed x3 -> x0, local copies, waits for them, and re-layouts: 4.21 us -> none
    pallas_call x0 -> x1, Pallas kernels: none -> 3 us  [shards(): pl.pallas_call(hand_over, out_shape=(jax.ShapeDtypeStruct((1, queries), F...]
    convert_element_type x2 -> x0, other arithmetic: 2.68 us -> none  [the longest x1 2.68 us: shards(): weight_grad.astype(F32)]
    pallas_call x1, Pallas kernels: 91.1 us -> 88.7 us  [shards(): pl.pallas_call(functools.partial(kernel, n_z, qlen, candidates.shape[1]),...]
    slice x1 -> x0, local copies, waits for them, and re-layouts: 1.32 us -> none  [shards(): loss[:, 0]]
where the time goes in v3:
time: 92.5 us; the launch traced here: 92.4 us
  Pallas kernels  91.7 us (99%)
    pallas_call x1, Pallas kernels, shards(): pl.pallas_call(functools.partial(kernel, n_z, qlen, candidates.shape[1]),...  88.7 us
    pallas_call x1, Pallas kernels, shards(): pl.pallas_call(hand_over, out_shape=(jax.ShapeDtypeStruct((1, queries), F...  3 us

profile of v3, /device:TPU:1, one launch (start us, length us, event | category | flops | bytes accessed | tf_op | source)
XLA Modules:
  0.0 92.4 jit_solution(11580442000781799076)
XLA Ops:
  0.6 88.7 %retriever.1 = (f32[1,128]{1,0:T(1,128)}, f32[512,128]{1,0:T(8,128)}, f32[768,128]{1,0:T(8,128)}, bf16[4096,128]{1,0:T(8,128)(2,1)}) custom-call(bf16[512,4096]{1,0:T(8,128)(2,1)} %bitcast.6, bf16[768,4096]{1,0:T(8,128)(2,1)} %bitcast.5, bf16[4096,128]{1,0:T(8,128)(2,1)} %proj_ref.1, s32[16,9]{1,0:T(8,128)} %cand_ref.1), custom_call_target="tpu_custom_call" | custom-call | tf_op jit(solution)/shard_map/retriever/pallas_call | solution.py:556
  89.4 3.0 %hand_over.1 = (f32[1,16]{1,0:T(1,128)}, f32[512,128]{1,0:T(8,128)}, f32[768,128]{1,0:T(8,128)}, f32[4096,128]{1,0:T(8,128)}) custom-call(f32[1,128]{1,0:T(1,128)} %get-tuple-element.12.loss_ref, f32[512,128]{1,0:T(8,128)} %get-tuple-element.13.qg_ref, f32[768,128]{1,0:T(8,128)} %get-tuple-element.14.pg_ref, bf16[4096,128]{1,0:T(8,128)(2,1)} %get-tuple-element.15.wg_ref), custom_call_target="tpu_custom_call" | custom-call | tf_op jit(solution)/shard_map/hand_over/pallas_call | solution.py:584

commit v4 on v3

--- a/solution.py
+++ b/solution.py
@@ -35,12 +35,13 @@
 
 
 def pick(k, values):
-    result = jnp.int32(values[0])
+    result = values[0]
     for i, v in enumerate(values[1:]):
-        result = jnp.where(k == i + 1, jnp.int32(v), result)
+        result = jnp.where(k == i + 1, v, result)
     return result
 
 
+FAR = [10, 9, 11, 6, 14, 2, 8, 5, 7, 13, 15, 1, 3, 4, 12]
 ORDER = [(0, 0), (1, 0), (3, 0), (0, 1), (0, 3), (1, 1), (1, 3), (3, 1), (3, 3),
          (2, 0), (0, 2), (2, 1), (2, 3), (1, 2), (3, 2), (2, 2)]
 
@@ -48,7 +49,7 @@
 def kernel(n_z, qlen, cand_count,
            qh_ref, ph_ref, proj_ref, cand_ref,
            loss_ref, qg_ref, pg_ref, wg_ref,
-           qh, ph, qe, pe, pt, pone, gq, ex, gn, qn, acc, cbuf, mask, mark, score, gsrep,
+           proj, qh, ph, qe, pe, pt, pone, gq, ex, gn, qn, acc, cbuf, mask, mark, score, gsrep,
            sbuf1, sbuf2, rbuf1, rbuf2, sum1, gp, qgb, pgb,
            wg, out, half, got0, part, got1, mine, got2,
            sem_h, c_s, c_r, sc_s, sc_r, a_s, a_r, b_s, b_r,
@@ -60,18 +61,26 @@
     queries = rows_q // qlen
     n_p, plen = pone.shape[0], pone.shape[1]
     width = qh.shape[1]
-    vec = proj_ref.shape[1]
+    vec = proj.shape[1]
     me, pb = lax.axis_index("pa"), lax.axis_index("pb")
     y, x = me // SIDE, me % SIDE
     z, core = pb // 2, pb % 2
     partner = {"pb": z * 2 + (1 - core)}
     scale = 1.0 / (vec * sharpness_divisor)
 
-    def xy(k):
-        return lax.rem(me + k, n_pa)
-
-    def zz(k):
-        return lax.rem(z + k, n_z)
+    rows = [lax.rem(y + d, SIDE) * SIDE for d in range(SIDE)]
+    columns = [lax.rem(x + d, SIDE) for d in range(SIDE)]
+    at_offset = [rows[k // SIDE] + columns[k % SIDE] for k in range(n_pa)]
+    along_z = [lax.rem(z + k, n_z) for k in range(n_z)]
+
+    def back(k):
+        return (SIDE - k // SIDE) % SIDE * SIDE + (SIDE - k % SIDE) % SIDE
+
+    def plane(k):
+        return {"pa": at_offset[k]}
+
+    def line_z(k):
+        return {"pb": along_z[k] * 2 + core}
 
     def load_q(k):
         at = pl.ds(k * hrow, hrow)
@@ -81,52 +90,49 @@
         at = pl.ds(k * plen, plen)
         return pltpu.make_async_copy(ph_ref.at[at], ph.at[at], sem_h.at[2 + k])
 
+    load_w = pltpu.make_async_copy(proj_ref, proj, sem_h.at[2 + n_p])
+    load_w.start()
     for k in range(2):
         load_q(k).start()
+
+    barrier = pltpu.get_barrier_semaphore()
+    pl.semaphore_signal(barrier, inc=1, device_id=partner, device_id_type=MESH)
+
+    for k in range(1, n_pa):
+        pl.semaphore_signal(barrier, inc=1, device_id=plane(k), device_id_type=MESH)
+    for k in range(1, n_z):
+        pl.semaphore_signal(barrier, inc=1, device_id=line_z(k), device_id_type=MESH)
+
     for k in range(n_p):
         load_p(k).start()
-
-    barrier = pltpu.get_barrier_semaphore()
-    pl.semaphore_signal(barrier, inc=1, device_id=partner, device_id_type=MESH)
-
-    @pl.loop(1, n_pa)
-    def _(k):
-        pl.semaphore_signal(barrier, inc=1, device_id={"pa": xy(k)}, device_id_type=MESH)
-
-    @pl.loop(1, n_z)
-    def _(k):
-        pl.semaphore_signal(barrier, inc=1, device_id={"pb": zz(k) * 2 + core}, device_id_type=MESH)
 
     lane = lax.broadcasted_iota(jnp.int32, (queries, 128), 1)
     line = lax.broadcasted_iota(jnp.int32, (queries, 128), 0)
     place = (lane == line + (me % 8) * queries).astype(F32)
-    cbuf[me] = jnp.zeros((16, 128), F32)
-    cbuf[me, 0:cand_count, :] = dot(cand_ref[...].astype(F32), place, 0, 0)
+    cbuf[me] = jnp.concatenate([dot(cand_ref[...].astype(F32), place, 0, 0), jnp.zeros((16 - cand_count, 128), F32)], axis=0).astype(BF16)
     score[...] = jnp.zeros_like(score)
     acc[...] = jnp.zeros_like(acc)
 
+    def shift(h, d1, d2):
+        dx, dy = (d1, d2) if h == 0 else (d2, d1)
+        return dy % SIDE * SIDE + dx % SIDE
+
     def slot(h, d1, d2):
-        dx, dy = d1 * (1 - h) + d2 * h, d2 * (1 - h) + d1 * h
-        return lax.rem(y + dy, SIDE) * SIDE + lax.rem(x + dx, SIDE)
-
-    def offset(h, g, o):
-        first = jnp.int32(g == 0) if isinstance(g, int) else (g == 0).astype(jnp.int32)
-        d1 = first * o + (1 - first) * (g - 1)
-        return d1, (1 - first) * o
+        return at_offset[shift(h, d1, d2)]
 
     def neighbour(h, g, o):
-        first = jnp.int32(g == 0) if isinstance(g, int) else (g == 0).astype(jnp.int32)
-        return {"pa": slot(h, first * o, (1 - first) * o)}
+        return plane(shift(h, o, 0) if g == 0 else shift(h, 0, o))
+
+    def piece_of(h, g, o, k, to, first, count):
+        d1, d2 = (o, 0) if g == 0 else (g - 1, o)
+        block = gq.at[slot(h, d1, d2), pl.ds(h * hrow + first, count)]
+        return remote(block, block, a_s, a_r.at[(h * 5 + g) * 4 + k], neighbour(h, g, to))
 
     def whole(h, g, o, k, to):
-        block = gq.at[slot(h, *offset(h, g, o)), pl.ds(h * hrow, hrow)]
-        i = (h * 5 + g) * 4 + k
-        return remote(block, block, a_s.at[i], a_r.at[i], neighbour(h, g, to))
+        return piece_of(h, g, o, k, to, 0, hrow)
 
     def quarter(h, g, o, k, to):
-        block = gq.at[slot(h, *offset(h, g, o)), pl.ds(h * hrow + (k - 2) * qrow, qrow)]
-        i = (h * 5 + g) * 4 + k
-        return remote(block, block, a_s.at[i], a_r.at[i], neighbour(h, g, to))
+        return piece_of(h, g, o, k, to, (k - 2) * qrow, qrow)
 
     def send_whole(h, g):
         whole(h, g, 0, 0, 1).start()
@@ -142,22 +148,20 @@
         quarter(h, g, 2, 2, 1).wait_recv()
         quarter(h, g, 2, 3, 3).wait_recv()
 
-    def sent(h, g):
-        whole(h, g, 0, 0, 1).wait_send()
-        whole(h, g, 0, 1, 3).wait_send()
-        quarter(h, g, 3, 2, 1).wait_send()
-        quarter(h, g, 1, 3, 3).wait_send()
-
-    def to_all(buf, send, recv, k):
-        return remote(buf.at[me], buf.at[me], send.at[k], recv.at[n_pa - k], {"pa": xy(k)})
-
-    def from_all(buf, send, recv, k):
-        return remote(buf.at[xy(k)], buf.at[xy(k)], send.at[k], recv.at[k], {"pa": xy(k)})
+    def to_all(buf, send, recv):
+        for k in FAR:
+            remote(buf.at[me], buf.at[me], send, recv, plane(k)).start()
+
+    def many(buf, count, send, recv):
+        part_of = buf.at[pl.ds(0, count)]
+        return remote(part_of, part_of, send, recv, partner)
 
     for h in range(2):
         at = pl.ds(h * hrow, hrow)
+        if h == 0:
+            load_w.wait()
         load_q(h).wait()
-        e = dot(qh[at, :], proj_ref[...])
+        e = dot(qh[at, :], proj[...])
         qe[at, :] = e
         gq[me, at, :] = (e * inverse_norm(e)).astype(BF16)
         if h == 0:
@@ -165,14 +169,12 @@
         send_whole(h, 0)
         send_whole(h, 1)
 
-    @pl.loop(1, n_pa)
-    def _(k):
-        to_all(cbuf, c_s, c_r, k).start()
+    to_all(cbuf, c_s, c_r)
 
     def project_passage(k):
         load_p(k).wait()
         at = pl.ds(k * plen, plen)
-        e = dot(ph[at, :], proj_ref[...])
+        e = dot(ph[at, :], proj[...])
         pe[at, :] = e
         u = (e * inverse_norm(e)).astype(BF16)
         pone[k, :, 0:vec] = u
@@ -181,16 +183,14 @@
 
     project_passage(0)
 
-    @pl.loop(0, 2)
-    def _(h):
+    for h in range(2):
         pass_on(h, 0)
         send_whole(h, 2)
         send_whole(h, 4)
 
     project_passage(1)
 
-    @pl.loop(0, 2)
-    def _(h):
+    for h in range(2):
         pass_on(h, 1)
 
     for k in range(2, n_p):
@@ -202,45 +202,38 @@
     def _(k):
         @pl.when(k == 2)
         def _():
-            @pl.loop(0, 2)
-            def _(h):
+            for h in range(2):
                 finish(h, 0)
                 send_whole(h, 3)
 
         @pl.when(k == 4)
         def _():
-            @pl.loop(0, 2)
-            def _(h):
+            for h in range(2):
                 pass_on(h, 2)
                 pass_on(h, 4)
 
         @pl.when(k == 7)
         def _():
-            @pl.loop(0, 2)
-            def _(h):
+            for h in range(2):
                 pass_on(h, 3)
 
         @pl.when(k == 9)
         def _():
-            @pl.loop(0, 2)
-            def _(h):
+            for h in range(2):
                 finish(h, 1)
 
         @pl.when(k == 11)
         def _():
-            @pl.loop(0, 2)
-            def _(h):
+            for h in range(2):
                 finish(h, 2)
                 finish(h, 4)
 
         @pl.when(k == 15)
         def _():
-            @pl.loop(0, 2)
-            def _(h):
+            for h in range(2):
                 finish(h, 3)
 
-        dx, dy = pick(k, [d[0] for d in ORDER]), pick(k, [d[1] for d in ORDER])
-        b = lax.rem(y + dy, SIDE) * SIDE + lax.rem(x + dx, SIDE)
+        b = pick(k, [at_offset[dy * SIDE + dx] for dx, dy in ORDER])
         u = gq[b]
         at = pl.ds(pl.multiple_of(b * rows_q, rows_q), rows_q)
         for p in range(n_p):
@@ -262,18 +255,13 @@
         for i in range(2):
             score[me, p:p + 1, i * 128:(i + 1) * 128] = sharpness_divisor * jnp.sum(acc[p, i], axis=0, keepdims=True)
 
-    @pl.loop(1, n_pa)
-    def _(k):
-        to_all(score, sc_s, sc_r, k).start()
-
-    @pl.loop(1, n_pa)
-    def _(k):
-        from_all(cbuf, c_s, c_r, k).wait_recv()
-
-    left, right = cbuf[0], cbuf[8]
+    to_all(score, sc_s, sc_r)
+    many(cbuf, n_pa - 1, c_s, c_r).wait_recv()
+
+    left, right = cbuf[0].astype(F32), cbuf[8].astype(F32)
     for i in range(1, 8):
-        left = left + cbuf[i]
-        right = right + cbuf[8 + i]
+        left = left + cbuf[i].astype(F32)
+        right = right + cbuf[8 + i].astype(F32)
     named = jnp.concatenate([left, right], axis=1).astype(jnp.int32)
     rank = lax.broadcasted_iota(jnp.int32, (8, 256), 0)
 
@@ -287,9 +275,7 @@
         mask[o] = found
         mark[o] = first
 
-    @pl.loop(1, n_pa)
-    def _(k):
-        from_all(score, sc_s, sc_r, k).wait_recv()
+    many(score, n_pa - 1, sc_s, sc_r).wait_recv()
 
     similarity = score[...]
     exponent = jnp.exp(similarity) * mask[...]
@@ -311,7 +297,7 @@
         return jnp.broadcast_to(g[:, None, :], (count, qlen, vec)).reshape(count * qlen, vec)
 
     def value(h, g, o):
-        if isinstance(g, int) and g == 0:
+        if g == 0:
             return sum1[h * SIDE + o]
         b = slot(h, g - 1, o)
         at = pl.ds(pl.multiple_of(b * rows_q + h * hrow, hrow), hrow)
@@ -323,11 +309,11 @@
     def leg1(h, g, k, to):
         i = h * 5 + g
         at = pl.ds(k * qrow, qrow)
-        return remote(sbuf1.at[i, at], rbuf1.at[i, at], b_s.at[i * 4 + k], b_r.at[i * 4 + k], neighbour(h, g, to))
+        return remote(sbuf1.at[i, at], rbuf1.at[i, at], b_s, b_r.at[i * 4 + k], neighbour(h, g, to))
 
     def leg2(h, g, k, to):
         i = h * 5 + g
-        return remote(sbuf2.at[i * 2 + k], rbuf2.at[i * 2 + k], b_s.at[i * 4 + 2 + k], b_r.at[i * 4 + 2 + k],
+        return remote(sbuf2.at[i * 2 + k], rbuf2.at[i * 2 + k], b_s, b_r.at[i * 4 + 2 + k],
                       neighbour(h, g, to))
 
     def step1(h, g):
@@ -366,33 +352,19 @@
 
     gp[...] = jnp.zeros_like(gp)
 
-    @pl.loop(0, 8)
-    def _(i):
-        step1(i % 2, 1 + lax.rem(i // 2 + 2, SIDE))
-
-    grad_passage(0, 3)
-
-    @pl.loop(0, 8)
-    def _(i):
-        step2(i % 2, 1 + lax.rem(i // 2 + 2, SIDE))
-
-    grad_passage(3, 9)
-
-    @pl.loop(0, 2)
-    def _(h):
+    for i in range(8):
+        step1(i % 2, 1 + (i // 2 + 2) % SIDE)
+
+    grad_passage(0, 5)
+
+    for i in range(8):
+        step2(i % 2, 1 + (i // 2 + 2) % SIDE)
+
+    grad_passage(5, 16)
+
+    for h in range(2):
         sum1[h * SIDE + 2] = step3(h, 3)
         step1(h, 0)
-
-    grad_passage(9, 12)
-
-    @pl.loop(0, 2)
-    def _(h):
-        sum1[h * SIDE + 1] = step3(h, 2)
-        sum1[h * SIDE + 3] = step3(h, 4)
-        sum1[h * SIDE] = step3(h, 1)
-        step2(h, 0)
-
-    grad_passage(12, 16)
 
     for p in range(n_p):
         at = pl.ds(p * plen, plen)
@@ -402,10 +374,21 @@
 
     quarter_rows = width // 8
 
-    @pl.loop(0, 8)
-    def _(c):
-        at = pl.ds(pl.multiple_of(c * quarter_rows, quarter_rows), quarter_rows)
-        wg[at, :] = dot(ph[:, at], pgb[...], 0, 0)
+    def passage_product(first, last):
+        @pl.loop(first, last)
+        def _(c):
+            at = pl.ds(pl.multiple_of(c * quarter_rows, quarter_rows), quarter_rows)
+            wg[at, :] = dot(ph[:, at], pgb[...], 0, 0)
+
+    passage_product(0, 3)
+
+    for h in range(2):
+        sum1[h * SIDE + 1] = step3(h, 2)
+        sum1[h * SIDE + 3] = step3(h, 4)
+        step2(h, 0)
+        sum1[h * SIDE] = step3(h, 1)
+
+    passage_product(3, 8)
 
     for h in range(2):
         at = pl.ds(h * hrow, hrow)
@@ -419,7 +402,7 @@
 
     def swap(j):
         at = pl.ds(pl.multiple_of(lax.rem(y + 1 + j, SIDE) * quarter_rows, quarter_rows), quarter_rows)
-        return remote(half.at[at], got0.at[at], s0.at[j], r0.at[j], partner)
+        return remote(half.at[at], got0.at[at], s0, r0.at[j], partner)
 
     def product(first, j):
         at = pl.ds(pl.multiple_of(first + lax.rem(y + 1 + j, SIDE) * quarter_rows, quarter_rows), quarter_rows)
@@ -431,8 +414,8 @@
         half[at, :] = product(half_rows - base, j).astype(BF16)
         swap(j).start()
 
-    def to_xy(k, peer):
-        return remote(part.at[peer], got1.at[me], s1.at[k], r1.at[n_pa - k], {"pa": peer})
+    def to_xy(peer):
+        return remote(part.at[peer], got1.at[me], s1, r1, {"pa": peer})
 
     @pl.loop(0, SIDE)
     def _(j):
@@ -447,90 +430,59 @@
             def _():
                 mine[...] = v[i * chunk:(i + 1) * chunk]
 
-        @pl.loop(1, SIDE + 1)
-        def _(i):
-            peer = row * SIDE + lax.rem(x + i, SIDE)
-
-            @pl.when(peer != me)
-            def _():
-                to_xy(lax.rem(peer + n_pa - me, n_pa), peer).start()
-
-    @pl.loop(1, n_pa)
-    def _(k):
-        remote(part.at[xy(k)], got1.at[xy(k)], s1.at[k], r1.at[k], {"pa": xy(k)}).wait_recv()
-        mine[...] += got1[xy(k)].astype(F32)
-
-    part[me] = mine[...].astype(BF16)
-    got2[z] = mine[...].astype(BF16)
-
-    def to_z(k, who, recv):
-        return remote(part.at[me], got2.at[who], s2.at[k], r2.at[recv], {"pb": zz(k) * 2 + core})
-
-    @pl.loop(1, n_z)
-    def _(k):
-        to_z(k, z, n_z - k).start()
-
-    @pl.loop(1, n_z)
-    def _(k):
-        to_z(k, zz(k), k).wait_recv()
-
+        for i in range(1, SIDE):
+            to_xy(row * SIDE + columns[i]).start()
+
+        @pl.when(j < SIDE - 1)
+        def _():
+            to_xy(row * SIDE + x).start()
+
+    many(got1, n_pa - 1, s1, r1).wait_recv()
+    total = mine[...]
+    for k in range(1, n_pa):
+        total = total + got1[at_offset[k]].astype(F32)
+    total = total.astype(BF16)
+    part[me] = total
+    got2[z] = total
+    for k in range(1, n_z):
+        remote(part.at[me], got2.at[z], s2, r2, line_z(k)).start()
+    if n_z > 1:
+        many(got2, n_z - 1, s2, r2).wait_recv()
     total = got2[0].astype(F32)
     for k in range(1, n_z):
         total = total + got2[k].astype(F32)
     out[pl.ds(base + me * chunk, chunk), :] = total.astype(BF16)
 
+    def chunk_at(first, who):
+        return out.at[pl.ds(first + who * chunk, chunk)]
+
     def back_xy(k, who, recv):
-        at = pl.ds(base + who * chunk, chunk)
-        return remote(out.at[at], out.at[at], s4.at[k], r4.at[recv], {"pa": xy(k)})
-
-    @pl.loop(1, n_pa)
-    def _(k):
-        back_xy(k, me, n_pa - k).start()
-
-    def across(k, first):
-        at = pl.ds(first + xy(k) * chunk, chunk)
-        return remote(out.at[at], out.at[at], s5.at[k], r5.at[k], partner)
-
-    across(0, base).start()
-
-    @pl.loop(1, n_pa)
-    def _(k):
-        back_xy(k, xy(k), k).wait_recv()
-        across(k, base).start()
-
-    @pl.loop(0, n_pa)
-    def _(k):
-        across(k, half_rows - base).wait_recv()
-
+        return remote(chunk_at(base, who), chunk_at(base, who), s4, r4.at[recv], plane(k))
+
+    def across(k):
+        here = chunk_at(base, at_offset[k])
+        return remote(here, here, s5, r5, partner)
+
+    for k in FAR:
+        back_xy(k, me, back(k)).start()
+    across(0).start()
+    for k in FAR[::-1]:
+        back_xy(k, at_offset[k], k).wait_recv()
+        across(k).start()
+    many(out, half_rows, s5, r5).wait_recv()
     wg_ref[...] = out[...]
 
-    @pl.loop(0, 10)
-    def _(i):
-        h, g = i // 5, lax.rem(i, 5)
-        sent(h, g)
-        leg1(h, g, 0, 1).wait_send()
-        leg1(h, g, 1, 3).wait_send()
-        leg2(h, g, 0, 1).wait_send()
-        leg2(h, g, 1, 3).wait_send()
-
-    @pl.loop(1, n_pa)
-    def _(k):
-        to_all(cbuf, c_s, c_r, k).wait_send()
-        to_all(score, sc_s, sc_r, k).wait_send()
-        to_xy(k, xy(k)).wait_send()
-        back_xy(k, me, n_pa - k).wait_send()
-
-    @pl.loop(1, n_z)
-    def _(k):
-        to_z(k, z, n_z - k).wait_send()
-
-    @pl.loop(0, SIDE)
-    def _(j):
-        swap(j).wait_send()
-
-    @pl.loop(0, n_pa)
-    def _(k):
-        across(k, base).wait_send()
+    many(gq, n_pa - 1, a_s, a_s).wait_send()
+    many(sbuf1, 10, b_s, b_s).wait_send()
+    many(sbuf2, 20, b_s, b_s).wait_send()
+    many(cbuf, n_pa - 1, c_s, c_r).wait_send()
+    many(score, n_pa - 1, sc_s, sc_r).wait_send()
+    many(half, half_rows, s0, s0).wait_send()
+    many(part, n_pa - 1, s1, r1).wait_send()
+    if n_z > 1:
+        many(got2, n_z - 1, s2, r2).wait_send()
+    many(out, chunk * (n_pa - 1), s4, s4).wait_send()
+    many(out, half_rows, s5, r5).wait_send()
 
 
 def hand_over(loss_ref, qg_ref, pg_ref, wg_ref, loss_out, qg_out, pg_out, wg_out):
@@ -561,22 +513,20 @@
             jax.ShapeDtypeStruct((rows_p, vec), F32),
             jax.ShapeDtypeStruct((width, vec), BF16),
         ),
-        in_specs=[anywhere, anywhere, in_vmem, in_vmem],
+        in_specs=[anywhere, anywhere, anywhere, in_vmem],
         out_specs=(in_vmem,) * 4,
         scratch_shapes=[
-            V((rows_q, width), BF16), V((rows_p, width), BF16), V((rows_q, vec), F32), V((rows_p, vec), F32),
+            V((width, vec), BF16), V((rows_q, width), BF16), V((rows_p, width), BF16), V((rows_q, vec), F32), V((rows_p, vec), F32),
             V((n_p, vec, plen), BF16), V((n_p, plen, 2 * vec), BF16), V((n_pa, rows_q, vec), BF16),
             V((n_p, all_rows, plen), BF16), V((n_p, all_rows, vec), BF16), V((n_p, all_rows, vec), BF16),
-            V((n_p, 2, 8, 128), F32), V((n_pa, 16, 128), F32), V((n_pa, 8, 256), F32), V((n_pa, 8, 256), F32),
+            V((n_p, 2, 8, 128), F32), V((n_pa, 16, 128), BF16), V((n_pa, 8, 256), F32), V((n_pa, 8, 256), F32),
             V((n_pa, 8, 256), F32), V((n_p, 256, vec), F32),
             V((10, hrow, vec), BF16), V((20, hrow, vec), BF16), V((10, hrow, vec), BF16), V((20, hrow, vec), BF16),
             V((2 * SIDE, hrow, vec), F32), V((n_p, plen, vec), F32), V((rows_q, vec), BF16), V((rows_p, vec), BF16),
             V((width, vec), F32), V((width, vec), BF16), V((half_rows, vec), BF16), V((half_rows, vec), BF16),
             V((n_pa, chunk, vec), BF16), V((n_pa, chunk, vec), BF16), V((chunk, vec), F32), V((n_z, chunk, vec), BF16),
-            dma((2 + n_p,)), dma((n_pa,)), dma((n_pa,)), dma((n_pa,)), dma((n_pa,)),
-            dma((40,)), dma((40,)), dma((40,)), dma((40,)),
-            dma((SIDE,)), dma((SIDE,)), dma((n_pa,)), dma((n_pa,)), dma((n_z,)), dma((n_z,)),
-            dma((n_pa,)), dma((n_pa,)), dma((n_pa,)), dma((n_pa,)),
+            dma((3 + n_p,)), dma, dma, dma, dma, dma, dma((40,)), dma, dma((40,)),
+            dma, dma((SIDE,)), dma, dma, dma, dma, dma, dma((n_pa,)), dma, dma,
         ],
         compiler_params=pltpu.CompilerParams(collective_id=0, has_side_effects=True, vmem_limit_bytes=60 * 2**20),
         name="retriever",

time: 92.5 us -> 88.5 us (0.957)
  Pallas kernels: 91.7 us -> 87.7 us
    pallas_call x1, Pallas kernels: 88.7 us -> 84.7 us  [shards(): pl.pallas_call(functools.partial(kernel, n_z, qlen, candidates.shape[1]),...]
where the time goes in v4:
time: 88.5 us; the launch traced here: 88.4 us
  Pallas kernels  87.7 us (99%)
    pallas_call x1, Pallas kernels, shards(): pl.pallas_call(functools.partial(kernel, n_z, qlen, candidates.shape[1]),...  84.7 us
    pallas_call x1, Pallas kernels, shards(): pl.pallas_call(hand_over, out_shape=(jax.ShapeDtypeStruct((1, queries), F...  3 us

profile of v4, /device:TPU:1, one launch (start us, length us, event | category | flops | bytes accessed | tf_op | source)
XLA Modules:
  0.0 88.4 jit_solution(2697951482715104848)
XLA Ops:
  0.6 84.7 %retriever.1 = (f32[1,128]{1,0:T(1,128)}, f32[512,128]{1,0:T(8,128)}, f32[768,128]{1,0:T(8,128)}, bf16[4096,128]{1,0:T(8,128)(2,1)}) custom-call(bf16[512,4096]{1,0:T(8,128)(2,1)} %bitcast.6, bf16[768,4096]{1,0:T(8,128)(2,1)} %bitcast.5, bf16[4096,128]{1,0:T(8,128)(2,1)} %proj_ref.1, s32[16,9]{1,0:T(8,128)} %cand_ref.1), custom_call_target="tpu_custom_call" | custom-call | tf_op jit(solution)/shard_map/retriever/pallas_call | solution.py:508
  85.4 3.0 %hand_over.1 = (f32[1,16]{1,0:T(1,128)}, f32[512,128]{1,0:T(8,128)}, f32[768,128]{1,0:T(8,128)}, f32[4096,128]{1,0:T(8,128)}) custom-call(f32[1,128]{1,0:T(1,128)} %get-tuple-element.12.loss_ref, f32[512,128]{1,0:T(8,128)} %get-tuple-element.13.qg_ref, f32[768,128]{1,0:T(8,128)} %get-tuple-element.14.pg_ref, bf16[4096,128]{1,0:T(8,128)(2,1)} %get-tuple-element.15.wg_ref), custom_call_target="tpu_custom_call" | custom-call | tf_op jit(solution)/shard_map/hand_over/pallas_call | solution.py:534

commit v5 on v4

--- a/solution.py
+++ b/solution.py
@@ -150,7 +150,11 @@
 
     def to_all(buf, send, recv):
         for k in FAR:
-            remote(buf.at[me], buf.at[me], send, recv, plane(k)).start()
+            remote(buf, buf, send, recv, plane(k)).start()
+
+    def scores_in():
+        part_of = score.at[pl.ds(0, n_pa - 1), pl.ds(0, 4)]
+        return remote(part_of, part_of, sc_s, sc_r, partner)
 
     def many(buf, count, send, recv):
         part_of = buf.at[pl.ds(0, count)]
@@ -169,7 +173,7 @@
         send_whole(h, 0)
         send_whole(h, 1)
 
-    to_all(cbuf, c_s, c_r)
+    to_all(cbuf.at[me], c_s, c_r)
 
     def project_passage(k):
         load_p(k).wait()
@@ -200,19 +204,19 @@
 
     @pl.loop(0, n_pa)
     def _(k):
-        @pl.when(k == 2)
+        @pl.when(k == 3)
         def _():
             for h in range(2):
                 finish(h, 0)
                 send_whole(h, 3)
 
-        @pl.when(k == 4)
+        @pl.when(k == 5)
         def _():
             for h in range(2):
                 pass_on(h, 2)
                 pass_on(h, 4)
 
-        @pl.when(k == 7)
+        @pl.when(k == 9)
         def _():
             for h in range(2):
                 pass_on(h, 3)
@@ -255,7 +259,7 @@
         for i in range(2):
             score[me, p:p + 1, i * 128:(i + 1) * 128] = sharpness_divisor * jnp.sum(acc[p, i], axis=0, keepdims=True)
 
-    to_all(score, sc_s, sc_r)
+    to_all(score.at[me, pl.ds(0, 4)], sc_s, sc_r)
     many(cbuf, n_pa - 1, c_s, c_r).wait_recv()
 
     left, right = cbuf[0].astype(F32), cbuf[8].astype(F32)
@@ -275,7 +279,7 @@
         mask[o] = found
         mark[o] = first
 
-    many(score, n_pa - 1, sc_s, sc_r).wait_recv()
+    scores_in().wait_recv()
 
     similarity = score[...]
     exponent = jnp.exp(similarity) * mask[...]
@@ -348,7 +352,7 @@
             at = pl.ds(pl.multiple_of(b * rows_q, rows_q), rows_q)
             for p in range(n_p):
                 w = (spread(p, b, 0, queries) * qn[p, at, :].astype(F32)).astype(BF16)
-                gp[p] += dot(ex[p, at, :], w, 0, 0)
+                gp[p] += dot(w.T, ex[p, at, :])
 
     gp[...] = jnp.zeros_like(gp)
 
@@ -368,9 +372,9 @@
 
     for p in range(n_p):
         at = pl.ds(p * plen, plen)
-        g = norm_backward(pe[at, :], gp[p])
+        g = norm_backward(pe[at, :], gp[p].T)
         pg_ref[at, :] = g
-        pgb[at, :] = g.astype(BF16)
+        pgb[:, at] = g.T.astype(BF16)
 
     quarter_rows = width // 8
 
@@ -378,7 +382,7 @@
         @pl.loop(first, last)
         def _(c):
             at = pl.ds(pl.multiple_of(c * quarter_rows, quarter_rows), quarter_rows)
-            wg[at, :] = dot(ph[:, at], pgb[...], 0, 0)
+            wg[at, :] = dot(pgb[...], ph[:, at]).T
 
     passage_product(0, 3)
 
@@ -394,7 +398,7 @@
         at = pl.ds(h * hrow, hrow)
         g = norm_backward(qe[at, :], step3(h, 0))
         qg_ref[at, :] = g
-        qgb[at, :] = g.astype(BF16)
+        qgb[:, at] = g.T.astype(BF16)
 
     half_rows = width // 2
     chunk = half_rows // n_pa
@@ -406,7 +410,7 @@
 
     def product(first, j):
         at = pl.ds(pl.multiple_of(first + lax.rem(y + 1 + j, SIDE) * quarter_rows, quarter_rows), quarter_rows)
-        return wg[at, :] + dot(qh[:, at], qgb[...], 0, 0)
+        return wg[at, :] + dot(qgb[...], qh[:, at]).T
 
     @pl.loop(0, SIDE)
     def _(j):
@@ -476,7 +480,7 @@
     many(sbuf1, 10, b_s, b_s).wait_send()
     many(sbuf2, 20, b_s, b_s).wait_send()
     many(cbuf, n_pa - 1, c_s, c_r).wait_send()
-    many(score, n_pa - 1, sc_s, sc_r).wait_send()
+    scores_in().wait_send()
     many(half, half_rows, s0, s0).wait_send()
     many(part, n_pa - 1, s1, r1).wait_send()
     if n_z > 1:
@@ -522,7 +526,7 @@
             V((n_p, 2, 8, 128), F32), V((n_pa, 16, 128), BF16), V((n_pa, 8, 256), F32), V((n_pa, 8, 256), F32),
             V((n_pa, 8, 256), F32), V((n_p, 256, vec), F32),
             V((10, hrow, vec), BF16), V((20, hrow, vec), BF16), V((10, hrow, vec), BF16), V((20, hrow, vec), BF16),
-            V((2 * SIDE, hrow, vec), F32), V((n_p, plen, vec), F32), V((rows_q, vec), BF16), V((rows_p, vec), BF16),
+            V((2 * SIDE, hrow, vec), F32), V((n_p, vec, plen), F32), V((vec, rows_q), BF16), V((vec, rows_p), BF16),
             V((width, vec), F32), V((width, vec), BF16), V((half_rows, vec), BF16), V((half_rows, vec), BF16),
             V((n_pa, chunk, vec), BF16), V((n_pa, chunk, vec), BF16), V((chunk, vec), F32), V((n_z, chunk, vec), BF16),
             dma((3 + n_p,)), dma, dma, dma, dma, dma, dma((40,)), dma, dma((40,)),

time: 88.5 us -> 86.9 us (0.982)
  Pallas kernels: 87.7 us -> 86.1 us
    pallas_call x1, Pallas kernels: 84.7 us -> 83.1 us  [shards(): pl.pallas_call(functools.partial(kernel, n_z, qlen, candidates.shape[1]),...]
where the time goes in v5:
time: 86.9 us; the launch traced here: 86.8 us
  Pallas kernels  86.1 us (99%)
    pallas_call x1, Pallas kernels, shards(): pl.pallas_call(functools.partial(kernel, n_z, qlen, candidates.shape[1]),...  83.1 us
    pallas_call x1, Pallas kernels, shards(): pl.pallas_call(hand_over, out_shape=(jax.ShapeDtypeStruct((1, queries), F...  3 us

profile of v5, /device:TPU:1, one launch (start us, length us, event | category | flops | bytes accessed | tf_op | source)
XLA Modules:
  0.0 86.8 jit_solution(11259915000573161955)
XLA Ops:
  0.6 83.1 %retriever.1 = (f32[1,128]{1,0:T(1,128)}, f32[512,128]{1,0:T(8,128)}, f32[768,128]{1,0:T(8,128)}, bf16[4096,128]{1,0:T(8,128)(2,1)}) custom-call(bf16[512,4096]{1,0:T(8,128)(2,1)} %bitcast.6, bf16[768,4096]{1,0:T(8,128)(2,1)} %bitcast.5, bf16[4096,128]{1,0:T(8,128)(2,1)} %proj_ref.1, s32[16,9]{1,0:T(8,128)} %cand_ref.1), custom_call_target="tpu_custom_call" | custom-call | tf_op jit(solution)/shard_map/retriever/pallas_call | solution.py:512
  83.8 3.0 %hand_over.1 = (f32[1,16]{1,0:T(1,128)}, f32[512,128]{1,0:T(8,128)}, f32[768,128]{1,0:T(8,128)}, f32[4096,128]{1,0:T(8,128)}) custom-call(f32[1,128]{1,0:T(1,128)} %get-tuple-element.12.loss_ref, f32[512,128]{1,0:T(8,128)} %get-tuple-element.13.qg_ref, f32[768,128]{1,0:T(8,128)} %get-tuple-element.14.pg_ref, bf16[4096,128]{1,0:T(8,128)(2,1)} %get-tuple-element.15.wg_ref), custom_call_target="tpu_custom_call" | custom-call | tf_op jit(solution)/shard_map/hand_over/pallas_call | solution.py:538

commit v6 on v5

--- a/solution.py
+++ b/solution.py
@@ -187,16 +187,13 @@
 
     project_passage(0)
 
+    project_passage(1)
+
     for h in range(2):
         pass_on(h, 0)
         send_whole(h, 2)
         send_whole(h, 4)
 
-    project_passage(1)
-
-    for h in range(2):
-        pass_on(h, 1)
-
     for k in range(2, n_p):
         project_passage(k)
 
@@ -204,6 +201,11 @@
 
     @pl.loop(0, n_pa)
     def _(k):
+        @pl.when(k == 1)
+        def _():
+            for h in range(2):
+                pass_on(h, 1)
+
         @pl.when(k == 3)
         def _():
             for h in range(2):

time: 86.9 us -> 86.9 us (level)
  no operation moved by 1% of the time
where the time goes in v6:
time: 86.9 us; the launch traced here: 86.7 us
  Pallas kernels  86.1 us (99%)
    pallas_call x1, Pallas kernels, shards(): pl.pallas_call(functools.partial(kernel, n_z, qlen, candidates.shape[1]),...  83.1 us
    pallas_call x1, Pallas kernels, shards(): pl.pallas_call(hand_over, out_shape=(jax.ShapeDtypeStruct((1, queries), F...  3 us

profile of v6, /device:TPU:1, one launch (start us, length us, event | category | flops | bytes accessed | tf_op | source)
XLA Modules:
  0.0 86.7 jit_solution(6518702551983953389)
XLA Ops:
  0.6 83.1 %retriever.1 = (f32[1,128]{1,0:T(1,128)}, f32[512,128]{1,0:T(8,128)}, f32[768,128]{1,0:T(8,128)}, bf16[4096,128]{1,0:T(8,128)(2,1)}) custom-call(bf16[512,4096]{1,0:T(8,128)(2,1)} %bitcast.6, bf16[768,4096]{1,0:T(8,128)(2,1)} %bitcast.5, bf16[4096,128]{1,0:T(8,128)(2,1)} %proj_ref.1, s32[16,9]{1,0:T(8,128)} %cand_ref.1), custom_call_target="tpu_custom_call" | custom-call | tf_op jit(solution)/shard_map/retriever/pallas_call | solution.py:514
  83.7 3.0 %hand_over.1 = (f32[1,16]{1,0:T(1,128)}, f32[512,128]{1,0:T(8,128)}, f32[768,128]{1,0:T(8,128)}, f32[4096,128]{1,0:T(8,128)}) custom-call(f32[1,128]{1,0:T(1,128)} %get-tuple-element.12.loss_ref, f32[512,128]{1,0:T(8,128)} %get-tuple-element.13.qg_ref, f32[768,128]{1,0:T(8,128)} %get-tuple-element.14.pg_ref, bf16[4096,128]{1,0:T(8,128)(2,1)} %get-tuple-element.15.wg_ref), custom_call_target="tpu_custom_call" | custom-call | tf_op jit(solution)/shard_map/hand_over/pallas_call | solution.py:540
